TPU v7x, 512 devices: a whole 4x4x16 slice. The times are simulated.
512 devices in a mesh: dp: 32 (over z, x_lo), mp: 16 (over y, x_hi, core).
Axes of the slice: x: 4 (x_hi: 2, x_lo: 2; x = x_hi * 2 + x_lo), y: 4, z: 16, core: 2. Of those that a mesh axis runs over, the one named last changes fastest.
Arguments:
- tokens: bfloat16 [192, 8192], P(None, ('dp', 'mp')), may hold values from -6 to 6
- out_grad: bfloat16 [192, 8192], P(None, ('dp', 'mp')), may hold values from -6 to 6
- gate_weight: bfloat16 [28672, 8192], P(('dp', 'mp')), may hold values from -0.0625 to 0.0625
- up_weight: bfloat16 [28672, 8192], P(('dp', 'mp')), may hold values from -0.0625 to 0.0625
- down_weight: bfloat16 [28672, 8192], P(('dp', 'mp')), may hold values from -0.03125 to 0.03125
- input_proj: bfloat16 [64, 8192], replicated, may hold values from -0.0625 to 0.0625
- output_proj: bfloat16 [64, 8192], replicated, may hold values from -0.0625 to 0.0625
- gate_proj: bfloat16 [28672, 64], P(('dp', 'mp')), may hold values from -0.03125 to 0.03125
- up_proj: bfloat16 [28672, 64], P(('dp', 'mp')), may hold values from -0.03125 to 0.03125
- hidden_proj: bfloat16 [28672, 64], P(('dp', 'mp')), may hold values from -0.03125 to 0.03125
- doc_ids: int32 [192], replicated, may hold values from 0 to 7, never falling along the last dimension, each value on 1 to 48 neighbouring positions
Outputs:
- doc_grads: float32 [3, 8, 4096], replicated
Inputs may be any that keep to these rules, and one draw needn't show every extreme that they name: doc_ids never fall along the tokens; each document has 1 to 48 tokens and one has exactly that many.
All inputs are finite; a program needn't handle non-finite values.
Results may differ from a plain program's by a relative error of at most 0.003.
Values may be sent and summed in bfloat16 or wider, within the bound.
No kernel may reach another device: no remote copies, remote signals or barrier semaphores. Data moves between devices by JAX's collectives and lax.ppermute only.
A program may use at most 64 MiB of HBM per device.

v0:
```python
import jax
import jax.numpy as jnp
from jax import lax
from jax.sharding import PartitionSpec as P

DOCS = 8


def outer_docs(left_side, right_side, onehot):
    weighted = (onehot[:, :, None] * left_side[:, None, :]).reshape(left_side.shape[0], -1)
    blocks = jnp.dot(
        weighted.T, right_side, precision=lax.Precision.HIGHEST, preferred_element_type=jnp.float32
    )
    return blocks.reshape(onehot.shape[1], -1)


def by_rows(left_side, right_side):
    return lax.dot_general(
        left_side, right_side, (((1,), (1,)), ((), ())), preferred_element_type=jnp.float32
    )


def local(
    tokens,
    out_grad,
    gate_weight,
    up_weight,
    down_weight,
    input_proj,
    output_proj,
    gate_proj,
    up_proj,
    hidden_proj,
    doc_ids,
):
    tokens_all, grads_all = (
        lax.all_gather(tokens, ("dp", "mp"), axis=1, tiled=True),
        lax.all_gather(out_grad, ("dp", "mp"), axis=1, tiled=True),
    )
    gate_sum = by_rows(tokens_all, gate_weight)
    up_sum = by_rows(tokens_all, up_weight)
    hidden_grad = by_rows(grads_all, down_weight)
    in_factor = by_rows(tokens_all, input_proj)
    down_out = by_rows(grads_all, output_proj)
    sigmoid_gate = jax.nn.sigmoid(gate_sum)
    silu_gate = gate_sum * sigmoid_gate
    hidden = (silu_gate * up_sum).astype(jnp.bfloat16)
    gate_grad = (
        hidden_grad * up_sum * sigmoid_gate * (1.0 + gate_sum * (1.0 - sigmoid_gate))
    ).astype(jnp.bfloat16)
    up_grad = (hidden_grad * silu_gate).astype(jnp.bfloat16)
    gate_out = jnp.dot(gate_grad, gate_proj, preferred_element_type=jnp.float32)
    up_out = jnp.dot(up_grad, up_proj, preferred_element_type=jnp.float32)
    down_in = jnp.dot(hidden, hidden_proj, preferred_element_type=jnp.float32)
    onehot = (doc_ids[:, None] == jnp.arange(DOCS, dtype=jnp.int32)[None, :]).astype(jnp.float32)
    gate_out, up_out, down_in = lax.psum((gate_out, up_out, down_in), ("dp", "mp"))
    return jnp.stack(
        [
            outer_docs(gate_out, in_factor, onehot),
            outer_docs(up_out, in_factor, onehot),
            outer_docs(down_out, down_in, onehot),
        ]
    )


def solution(mesh):
    return jax.shard_map(
        local,
        mesh=mesh,
        in_specs=(
            P(None, ("dp", "mp")),
            P(None, ("dp", "mp")),
            P(("dp", "mp"), None),
            P(("dp", "mp"), None),
            P(("dp", "mp"), None),
            P(),
            P(),
            P(("dp", "mp"), None),
            P(("dp", "mp"), None),
            P(("dp", "mp"), None),
            P(),
        ),
        out_specs=P(),
        check_vma=False,
    )
```

profile of v0, /device:TPU:1, one launch (start us, length us, event | category | flops | bytes accessed | tf_op | source)
XLA Modules:
  0.0 2104.7 jit_solution(7828756745615787319)
XLA Ops:
  6.5 0.0 copy-start
  6.5 0.0 copy-start.4
  6.5 0.0 all-gather.5.cloned.1.call-start
  6.5 0.7 all-gather.5.cloned.1.call-update
  7.3 0.0 all-gather.3.cloned.1.call-start
  7.3 0.7 all-gather.3.cloned.1.call-update
  8.0 0.0 all-reduce.3.cloned.1.call-start
  8.1 0.7 fusion.6
  8.7 0.0 copy-start.7
  8.7 0.0 copy-start.5
  8.7 812.4 %all-gather.5.cloned.1.call-done = bf16[192,8192]{0,1:T(8,128)(2,1)} async-done(((bf16[192,16]{0,1:T(8,128)(2,1)}), bf16[192,8192]{0,1:T(8,128)(2,1)}) %all-gather.5.cloned.1.call-update) | async-done | bytes 3145744 | tf_op jit(solution)/shard_map/all_gather | solution.py:37
  821.2 3.2 fusion.12
  824.4 0.0 copy-start.8
  824.4 0.0 copy-start.9
  824.5 805.6 %all-gather.3.cloned.1.call-done = bf16[192,8192]{0,1:T(8,128)(2,1)} async-done(((bf16[192,16]{0,1:T(8,128)(2,1)}), bf16[192,8192]{0,1:T(8,128)(2,1)}) %all-gather.3.cloned.1.call-update) | async-done | bytes 3145744 | tf_op jit(solution)/shard_map/all_gather | solution.py:38
  1630.0 0.0 copy-done.4
  1630.0 0.0 copy-start.1
  1630.0 3.1 fusion.10
  1633.2 0.0 copy-done.7
  1633.2 0.8 fusion.1
  1634.0 0.0 copy-done.5
  1634.0 0.0 copy-done.1
  1634.0 0.8 fusion.11
  1634.8 0.0 copy-done.8
  1634.9 0.0 copy-start.3
  1634.9 0.8 fusion.3
  1635.7 0.0 copy-done.9
  1635.7 0.9 fusion.2
  1636.6 0.0 all-reduce.3.cloned.1.call-update
  1636.6 0.0 copy-done
  1636.6 0.0 copy-start.2
  1636.6 3.1 fusion.17
  1639.7 0.0 copy-done.3
  1639.8 0.3 copy-done.2
  1640.0 0.8 fusion.16
  1640.9 453.4 %all-reduce.3.cloned.1.call-done = (f32[192,64]{1,0:T(8,128)}, f32[192,64]{0,1:T(8,128)}, f32[192,64]{0,1:T(8,128)}) async-done(((f32[192,64]{1,0:T(8,128)}, f32[192,64]{0,1:T(8,128)}, f32[192,64]{0,1:T(8,128)}), (f32[192,64]{1,0:T(8,128)}, f32[192,64]{0,1:T(8,128)}, f32[192,64]{0,1:T(8,128)})) %all-reduce.3.cloned.1.call-update) | async-done | bytes 147472 | tf_op jit(solution)/shard_map/psum | solution.py:56
  2094.3 0.0 copy-start.6
  2094.3 1.1 broadcast_multiply_fusion.2
  2095.4 0.6 fusion.13
  2095.9 0.1 stack_reshape.9
  2096.1 0.6 fusion.14
  2096.6 0.1 stack_reshape.10
  2096.7 0.0 copy-done.6
  2096.7 0.6 fusion.15
  2097.3 0.1 stack_reshape.11
  2097.4 0.8 pad_maximum_fusion
Async XLA Ops:
  6.5 1630.0 %copy-start = (bf16[64,8192]{1,0:T(8,128)(2,1)S(1)}, bf16[64,8192]{1,0:T(8,128)(2,1)}, u32[]{:S(2)}) copy-start(bf16[64,8192]{1,0:T(8,128)(2,1)} %param.17) | copy-start | bytes 3145732
  6.5 1623.5 %copy-start.4 = (bf16[56,8192]{1,0:T(8,128)(2,1)S(1)}, bf16[56,8192]{1,0:T(8,128)(2,1)}, u32[]{:S(2)}) copy-start(bf16[56,8192]{1,0:T(8,128)(2,1)} %param.15) | copy-start | bytes 2752516
  6.5 814.6 %all-gather.5.cloned.1.call-start = ((), (), s32[]{:S(2)}) async-start(), calls=%async_computation.1 | async-start | bytes 4202496 | tf_op jit(solution)/shard_map/all_gather | solution.py:37
  7.3 1622.8 %all-gather.3.cloned.1.call-start = ((), (), s32[]{:S(2)}) async-start(), calls=%async_computation | async-start | bytes 4202496 | tf_op jit(solution)/shard_map/all_gather | solution.py:38
  8.0 2086.3 %all-reduce.3.cloned.1.call-start = ((), (), s32[]{:S(2)}) async-start(), calls=%async_computation.2 | async-start | bytes 458752 | tf_op jit(solution)/shard_map/psum | solution.py:56
  8.7 1624.5 %copy-start.7 = (bf16[56,64]{1,0:T(8,128)(2,1)S(1)}, bf16[56,64]{1,0:T(8,128)(2,1)}, u32[]{:S(2)}) copy-start(bf16[56,64]{1,0:T(8,128)(2,1)} %param.19) | copy-start | bytes 21508
  8.7 1625.3 %copy-start.5 = (bf16[56,8192]{1,0:T(8,128)(2,1)S(1)}, bf16[56,8192]{1,0:T(8,128)(2,1)}, u32[]{:S(2)}) copy-start(bf16[56,8192]{1,0:T(8,128)(2,1)} %param.14) | copy-start | bytes 2752516
  824.4 810.4 %copy-start.8 = (bf16[56,64]{1,0:T(8,128)(2,1)S(1)}, bf16[56,64]{1,0:T(8,128)(2,1)}, u32[]{:S(2)}) copy-start(bf16[56,64]{1,0:T(8,128)(2,1)} %param.18) | copy-start | bytes 21508
  824.4 811.3 %copy-start.9 = (bf16[56,64]{1,0:T(8,128)(2,1)S(1)}, bf16[56,64]{1,0:T(8,128)(2,1)}, u32[]{:S(2)}) copy-start(bf16[56,64]{1,0:T(8,128)(2,1)} %param.20) | copy-start | bytes 21508
  1630.0 4.0 copy-start.1
  1634.9 4.9 copy-start.3
  1636.6 3.5 copy-start.2
  2094.3 2.5 copy-start.6
Sparse Core Ops, SparseCore 0:
  9.6 811.5 all-gather.4
  823.4 806.6 all-gather.2
  1636.7 457.5 all-reduce.2
where the time goes:
time: 2110 us; the launch traced here: 2100 us
  waiting for transfers between devices  2070 us (98%)
    all_gather x1, waiting for transfers between devices, local(): lax.all_gather(tokens, ('dp', 'mp'), axis=1, tiled=True)  812 us
    all_gather x1, waiting for transfers between devices, local(): lax.all_gather(out_grad, ('dp', 'mp'), axis=1, tiled=True)  806 us
    psum x1, waiting for transfers between devices, local(): lax.psum((gate_out, up_out, down_in), ('dp', 'mp'))  453 us
  transfers between devices with their start and end apart: 3, of which 3 were waited for; matrix products, arithmetic and copies ran while one was open for 0% of the time, Pallas kernels for 0%

commit v1 on v0

v1 whole, which is shorter than its diff:
```python
import jax
import jax.numpy as jnp
from jax import lax
from jax.experimental import pallas as pl
from jax.experimental.pallas import tpu as pltpu
from jax.sharding import PartitionSpec as P

DOCS = 8
BOTH = ("dp", "mp")
NZ, NXL, NY, NXH, NC = 16, 2, 4, 2, 2
NX = NXL * NXH
PLANE = NX * NY
LOW = 32
HALF = 96
MIB = 1 << 20


def device(z, xl, y, xh, c):
    return (((z * NXL + xl) * NY + y) * NXH + xh) * NC + c


def along_x(z, y, c):
    return [device(z, xl, y, xh, c) for xl in range(NXL) for xh in range(NXH)]


def along_y(z, xl, xh, c):
    return [device(z, xl, y, xh, c) for y in range(NY)]


def x_groups(c):
    return [along_x(z, y, c) for z in range(NZ) for y in range(NY)]


def y_groups(c):
    return [along_y(z, xl, xh, c) for z in range(NZ) for xl in range(NXL) for xh in range(NXH)]


SITES = [(xl, y, xh) for xl in range(NXL) for y in range(NY) for xh in range(NXH)]
COLUMN_GROUPS = [[device(z, *s, c) for z in range(NZ) for c in range(NC)] for s in SITES]
Z_GROUPS = [[device(z, *s, c) for z in range(NZ)] for s in SITES for c in range(NC)]
FIRST_GROUPS = x_groups(0) + y_groups(1)
SECOND_GROUPS = y_groups(0) + x_groups(1)
PLANE_GROUPS = [[device(z, *s, c) for s in SITES] for z in range(NZ) for c in range(NC)]
LAYER_GROUPS = [[device(z, *s, c) for s in SITES for c in range(NC)] for z in range(NZ)]
PAIRS = [[2 * i, 2 * i + 1] for i in range(NZ * PLANE)]
SWAP = [(i, i ^ 1) for i in range(NZ * PLANE * NC)]


def exchange(blocks, groups):
    return lax.all_to_all(blocks, BOTH, 0, 0, axis_index_groups=groups)


def spread(block, groups):
    number = len(groups[0])
    return exchange(jnp.broadcast_to(block[None], (number,) + block.shape), groups)


def columns(a, b):
    return lax.dot_general(a, b, (((1,), (0,)), ((), ())), preferred_element_type=jnp.float32)


SLABS = 2


def block_kernel(core_ref, ga_ref, gb_ref, w_ref, pt_ref, f_ref, h_ref, x_ref, acc_ref, s_ref):
    step = pl.program_id(0)
    core = core_ref[0]
    lane16 = lax.broadcasted_iota(jnp.int32, (16, 128), 1)
    first = (lane16 < 64).astype(jnp.float32).astype(jnp.bfloat16)
    second = (lane16 >= 64).astype(jnp.float32).astype(jnp.bfloat16)
    for slab in range(SLABS):
        for place, (xl, y, xh) in enumerate(SITES):
            gx = xl * NXH + xh
            here, there = y * NX + gx, gx * NY + y
            q = here + core * (there - here)
            base = slab * 512 + place * 32
            x_ref[base : base + 32, 0:128] = ga_ref[q, slab * 32 : slab * 32 + 32, :]
            tile = gb_ref[q, slab * 16 : slab * 16 + 16, :]
            x_ref[base : base + 16, 128:256] = tile * first
            x_ref[base + 16 : base + 32, 128:256] = tile * second
    product = columns(w_ref[...], x_ref[...])

    @pl.when(step == 0)
    def _():
        acc_ref[...] = product

    @pl.when(step > 0)
    def _():
        acc_ref[...] += product

    @pl.when(step == pl.num_programs(0) - 1)
    def _():
        def rows(start, size, lanes):
            return acc_ref[start : start + size, lanes * 128 : lanes * 128 + 128]

        def both(start):
            return jnp.concatenate([rows(start, 56, 0), rows(start + 168, 56, 0)], axis=0)

        def grads(ranges):
            low = jnp.concatenate([rows(*r, 0) for r in ranges], axis=0)
            high = jnp.concatenate([rows(*r, 1) for r in ranges], axis=0)
            lane = lax.broadcasted_iota(jnp.int32, low.shape, 1)
            return jnp.where(lane < 64, pltpu.roll(low, 32, 1), high + pltpu.roll(high, 64, 1))

        gate_sum, up_sum = both(0), both(56)
        hidden_grad = grads([(112, 56), (280, 56)])
        sigmoid_gate = jax.nn.sigmoid(gate_sum)
        silu_gate = gate_sum * sigmoid_gate
        hidden = (silu_gate * up_sum).astype(jnp.bfloat16)
        gate_grad = (
            hidden_grad * up_sum * sigmoid_gate * (1.0 + gate_sum * (1.0 - sigmoid_gate))
        ).astype(jnp.bfloat16)
        up_grad = (hidden_grad * silu_gate).astype(jnp.bfloat16)
        s_ref[0:64] = columns(pt_ref[0], gate_grad)
        s_ref[64:128] = columns(pt_ref[1], up_grad)
        s_ref[128:192] = columns(pt_ref[2], hidden)
        for p in range(PLANE):
            f_ref[p, 0:8, :] = s_ref[p * 8 : p * 8 + 8, :]
            f_ref[p, 8:12, :] = s_ref[128 + p * 4 : 132 + p * 4, :]
            f_ref[p, 12:16, :] = jnp.zeros((4, 128), jnp.float32)
        h_ref[0:64] = rows(336, 64, 0)
        h_ref[64:128] = grads([(400, 64)])


def block(core, gathered, weights, projections):
    steps = NZ // SLABS
    return pl.pallas_call(
        block_kernel,
        grid=(steps,),
        in_specs=[
            pl.BlockSpec(memory_space=pltpu.SMEM),
            pl.BlockSpec((PLANE, 32 * SLABS, 128), lambda s: (0, s, 0)),
            pl.BlockSpec((PLANE, 16 * SLABS, 128), lambda s: (0, 512 // (16 * SLABS) + s, 0)),
            pl.BlockSpec((464, 512 * SLABS), lambda s: (0, s)),
            pl.BlockSpec((3, 64, 112), lambda s: (0, 0, 0)),
        ],
        out_specs=[
            pl.BlockSpec((PLANE, 16, 128), lambda s: (0, 0, 0)),
            pl.BlockSpec((128, 128), lambda s: (0, 0)),
        ],
        out_shape=[
            jax.ShapeDtypeStruct((PLANE, 16, 128), jnp.float32),
            jax.ShapeDtypeStruct((128, 128), jnp.float32),
        ],
        scratch_shapes=[
            pltpu.VMEM((512 * SLABS, 256), jnp.bfloat16),
            pltpu.VMEM((464, 256), jnp.float32),
            pltpu.VMEM((192, 128), jnp.float32),
        ],
        compiler_params=pltpu.CompilerParams(vmem_limit_bytes=24 * MIB),
        cost_estimate=pl.CostEstimate(
            flops=2 * 464 * 8192 * 256, bytes_accessed=12 * MIB, transcendentals=112 * 128
        ),
    )(core, gathered, gathered, weights, projections)


def outer_kernel(f_ref, h_ref, ids_ref, out_ref, s_ref):
    for p in range(PLANE):
        for c in range(NC):
            s_ref[p * 8 : p * 8 + 8, c * 128 : c * 128 + 128] = f_ref[p, c, 0:8, :]
            s_ref[128 + p * 4 : 132 + p * 4, c * 128 : c * 128 + 128] = f_ref[p, c, 8:12, :]
    known = jnp.concatenate([h_ref[0], h_ref[1]], axis=1)
    ids = ids_ref[...]
    sides = (
        (s_ref[0:64, :], known[0:64]),
        (s_ref[64:128, :], known[0:64]),
        (known[64:128], s_ref[128:192, :]),
    )
    for k, (left, right) in enumerate(sides):
        stacked = jnp.concatenate(
            [jnp.where(ids == d, left, 0.0) for d in range(DOCS)], axis=0
        )
        out_ref[k] = lax.dot_general(
            stacked,
            right,
            (((1,), (1,)), ((), ())),
            precision=lax.Precision.HIGHEST,
            preferred_element_type=jnp.float32,
        )


def outer(factors, known, ids):
    return pl.pallas_call(
        outer_kernel,
        out_shape=jax.ShapeDtypeStruct((3, DOCS * 64, 64), jnp.float32),
        scratch_shapes=[pltpu.VMEM((192, 256), jnp.float32)],
        compiler_params=pltpu.CompilerParams(vmem_limit_bytes=16 * MIB),
        cost_estimate=pl.CostEstimate(
            flops=2 * 3 * 512 * 256 * 64 * 6, bytes_accessed=2 * MIB, transcendentals=0
        ),
    )(factors, known, ids)


def local(
    tokens,
    out_grad,
    gate_weight,
    up_weight,
    down_weight,
    input_proj,
    output_proj,
    gate_proj,
    up_proj,
    hidden_proj,
    doc_ids,
):
    core = (lax.axis_index("mp") % NC).astype(jnp.int32).reshape(1)
    mine = tokens.T.reshape(16, NC, HALF)
    grads = out_grad.T.reshape(16, NC, HALF)
    wide = jnp.concatenate([grads[:, :, :LOW], mine], axis=2)
    rest = grads[:, :, LOW:].reshape(2, 8, NC, 64)
    rest = rest.transpose(1, 2, 0, 3).reshape(8, NC, 128)
    sent = jnp.concatenate([wide, rest], axis=0).transpose(1, 0, 2)
    sent = jnp.broadcast_to(sent[None], (NZ, NC, 24, 128)).reshape(NZ * NC, 24, 128)
    column = exchange(sent, COLUMN_GROUPS)
    wide = column[:, :16, :].reshape(512, 128)
    rest = column[:, 16:, :].reshape(NZ, NC, 8, 2, 64)
    rest = rest.transpose(0, 3, 2, 1, 4).reshape(256, 128)
    column = jnp.concatenate([wide, rest], axis=0)
    line = spread(column, FIRST_GROUPS)
    gathered = spread(line, SECOND_GROUPS).reshape(PLANE, 768, 128)

    own = jnp.concatenate([gate_weight, up_weight, down_weight], axis=0)
    weights = jnp.concatenate(
        [own, lax.ppermute(own, BOTH, SWAP), input_proj, output_proj], axis=0
    )
    turned = jnp.stack([gate_proj.T, up_proj.T, hidden_proj.T])
    turned = jnp.concatenate([turned, lax.ppermute(turned, BOTH, SWAP)], axis=2)

    factors, known = block(core, gathered, weights, turned)
    known = lax.all_gather(known, BOTH, axis=0, axis_index_groups=PAIRS)
    part = exchange(factors, PLANE_GROUPS).sum(0)
    part = spread(part, Z_GROUPS).sum(0)
    factors = spread(part, LAYER_GROUPS).reshape(PLANE, NC, 16, 128)
    ids = jnp.pad(doc_ids.reshape(NC, HALF), ((0, 0), (LOW, 0)), constant_values=-1)
    return outer(factors, known, ids.reshape(1, NC * 128)).reshape(3, DOCS, 4096)


def solution(mesh):
    return jax.shard_map(
        local,
        mesh=mesh,
        in_specs=(
            P(None, BOTH),
            P(None, BOTH),
            P(BOTH, None),
            P(BOTH, None),
            P(BOTH, None),
            P(),
            P(),
            P(BOTH, None),
            P(BOTH, None),
            P(BOTH, None),
            P(),
        ),
        out_specs=P(),
        check_vma=False,
    )
```

time: 2110 us -> 138 us (0.07)
  waiting for transfers between devices: 2070 us -> 33.3 us
  starting transfers between devices: 0.08 us -> 38.3 us
  blocking collectives: 0 us -> 30 us
  local copies, waits for them, and re-layouts: 0.68 us -> 22 us
    all_gather x2 -> x0, waiting for transfers between devices: 1620 us -> none  [the longest x1 812 us: local(): lax.all_gather(tokens, ('dp', 'mp'), axis=1, tiled=True)]
    psum x1 -> x0, waiting for transfers between devices: 453 us -> none  [local(): lax.psum((gate_out, up_out, down_in), ('dp', 'mp'))]
    all_to_all x0 -> x4, starting transfers between devices: none -> 34 us  [exchange(): return lax.all_to_all(blocks, BOTH, 0, 0, axis_index_groups=groups)]
    all_to_all x0 -> x4, waiting for transfers between devices: none -> 33.3 us  [exchange(): return lax.all_to_all(blocks, BOTH, 0, 0, axis_index_groups=groups)]
    all_to_all x0 -> x2, blocking collectives: none -> 28.1 us  [exchange(): return lax.all_to_all(blocks, BOTH, 0, 0, axis_index_groups=groups)]
  transfers between devices with their start and end apart: 3 -> 6, of which waited for: 3 -> 4; matrix products, arithmetic and copies ran while one was open for 0% -> 16% of each run, Pallas kernels for 0% -> 0%
where the time goes in v1:
time: 138 us; the launch traced here: 137 us
  starting transfers between devices  38.3 us (28%)
  waiting for transfers between devices  33.3 us (24%)
  blocking collectives  30 us (22%)
  local copies, waits for them, and re-layouts  22 us (16%)
  Pallas kernels  9.33 us (7%)
  other arithmetic  3.78 us (3%)
    all_to_all x4, starting transfers between devices, exchange(): return lax.all_to_all(blocks, BOTH, 0, 0, axis_index_groups=groups)  34 us
    all_to_all x4, waiting for transfers between devices, exchange(): return lax.all_to_all(blocks, BOTH, 0, 0, axis_index_groups=groups)  33.3 us
    all_to_all x2, blocking collectives, exchange(): return lax.all_to_all(blocks, BOTH, 0, 0, axis_index_groups=groups)  28.1 us
    unnamed x16, local copies, waits for them, and re-layouts  12.7 us
    pallas_call x1, Pallas kernels, block(): pl.pallas_call(block_kernel, grid=(steps,), in_specs=[pl.BlockSpec(memory...  7.92 us
    broadcast_in_dim x4, local copies, waits for them, and re-layouts, spread(): jnp.broadcast_to(block[None], (number,) + block.shape)  4.13 us
    concatenate x1, other arithmetic, local(): own = jnp.concatenate([gate_weight, up_weight, down_weight], axis=0)  3.53 us
  transfers between devices with their start and end apart: 6, of which 4 were waited for; matrix products, arithmetic and copies ran while one was open for 16% of the time, Pallas kernels for 0%

profile of v1, /device:TPU:1, one launch (start us, length us, event | category | flops | bytes accessed | tf_op | source)
XLA Modules:
  0.0 136.8 jit_solution(16638234119938358285)
XLA Ops:
  0.0 0.0 copy-start
  0.0 0.9 reshape.48
  0.9 0.1 slice.17
  1.0 0.1 reshape.51
  1.1 0.8 reshape.49
  1.9 0.1 maximum_bitcast_fusion
  2.0 0.7 broadcast_in_dim.10
  2.7 16.7 %all-to-all-start = ((bf16[32,24,128]{2,1,0:T(8,128)(2,1)}), bf16[32,24,128]{2,1,0:T(8,128)(2,1)S(1)}, u32[]{:S(2)}, u32[]{:S(2)}) async-start(bf16[32,24,128]{2,1,0:T(8,128)(2,1)} %bitcast.6), calls=%async_computation | async-start | bytes 393216 | tf_op jit(solution)/shard_map/all_to_all | solution.py:50
  19.4 3.5 %pad_maximum_fusion = bf16[168,8192]{1,0:T(8,128)(2,1)} fusion(bf16[56,8192]{1,0:T(8,128)(2,1)} %param.15, bf16[56,8192]{1,0:T(8,128)(2,1)} %param.14, bf16[56,8192]{1,0:T(8,128)(2,1)} %param.13), kind=kLoop, calls=%fused_computation | loop fusion | flops 8257536 | bytes 5505024 | tf_op jit(solution)/shard_map/concatenate | solution.py:223
  23.0 2.1 %collective-permute-start = (bf16[168,8192]{1,0:T(8,128)(2,1)}, bf16[168,8192]{1,0:T(8,128)(2,1)}, u32[]{:S(2)}, u32[]{:S(2)}) collective-permute-start(bf16[168,8192]{1,0:T(8,128)(2,1)} %pad_maximum_fusion), channel_id=1, source_target_pairs={{0,1},{1,0},{2,3},{3,2},{4,5},{5,4},{6,7},{7,6},{8,9},{9,8},{10,11... | collective-permute-start | bytes 8257544 | tf_op jit(solution)/shard_map/ppermute | solution.py:225
  25.1 0.8 copy.33
  25.9 0.8 copy.32
  26.7 0.8 copy.31
  27.6 2.2 %collective-permute-start.1 = (bf16[3,64,56]{2,1,0:T(8,128)(2,1)S(1)}, bf16[3,64,56]{2,1,0:T(8,128)(2,1)S(1)}, u32[]{:S(2)}, u32[]{:S(2)}) collective-permute-start(bf16[3,64,56]{2,1,0:T(8,128)(2,1)S(1)} %pad_maximum_fusion.2), channel_id=1, source_target_pairs={{0,1},{1,0},{2,3},{3,2},{4,5},{5,4},{6,7},{7,6},{8,9},{9,8},{10,11... | collective-permute-start | bytes 64520 | tf_op jit(solution)/shard_map/ppermute | solution.py:228
  29.7 2.2 %constant_dynamic-update-slice_fusion.5 = bf16[464,8192]{1,0:T(8,128)(2,1)} fusion(bf16[56,8192]{1,0:T(8,128)(2,1)} %param.13), kind=kLoop, calls=%fused_computation.9 | loop fusion | bytes 1835008
  31.9 0.0 copy-done
  31.9 1.0 constant_dynamic-update-slice_fusion.4
  33.0 5.1 %all-to-all-done = bf16[32,24,128]{2,1,0:T(8,128)(2,1)S(1)} async-done(((bf16[32,24,128]{2,1,0:T(8,128)(2,1)}), bf16[32,24,128]{2,1,0:T(8,128)(2,1)S(1)}, u32[]{:S(2)}, u32[]{:S(2)}) %all-to-all-start) | async-done | bytes 196640 | tf_op jit(solution)/shard_map/all_to_all | solution.py:50
  38.1 0.1 reshape.54
  38.2 0.1 copy.30
  38.3 0.1 reshape.55
  38.4 1.0 broadcast_in_dim.11
  39.5 4.2 %all-to-all-start.1 = ((bf16[4,768,128]{2,1,0:T(8,128)(2,1)}), bf16[4,768,128]{2,1,0:T(8,128)(2,1)S(1)}, u32[]{:S(2)}, u32[]{:S(2)}) async-start(bf16[4,768,128]{2,1,0:T(8,128)(2,1)} %broadcast_in_dim.11), calls=%async_computation.1 | async-start | bytes 1572864 | tf_op jit(solution)/shard_map/all_to_all | solution.py:50
  43.7 0.0 copy-done.1
  43.7 1.0 constant_dynamic-update-slice_fusion.3
  44.7 0.0 collective-permute-done.1
  44.7 0.1 pad_maximum_fusion.3.pt_ref
  44.8 7.5 %all-to-all-done.1 = bf16[4,768,128]{2,1,0:T(8,128)(2,1)S(1)} async-done(((bf16[4,768,128]{2,1,0:T(8,128)(2,1)}), bf16[4,768,128]{2,1,0:T(8,128)(2,1)S(1)}, u32[]{:S(2)}, u32[]{:S(2)}) %all-to-all-start.1) | async-done | bytes 786464 | tf_op jit(solution)/shard_map/all_to_all | solution.py:50
  52.3 2.4 %broadcast_in_dim.12 = bf16[4,4,768,128]{3,2,1,0:T(8,128)(2,1)} broadcast(bf16[4,768,128]{2,1,0:T(8,128)(2,1)S(1)} %all-to-all-done.1), dimensions={1,2,3} | broadcast | bytes 3932160 | tf_op jit(solution)/shard_map/broadcast_in_dim | solution.py:55
  54.7 3.7 %all-to-all-start.2 = ((bf16[4,4,768,128]{3,2,1,0:T(8,128)(2,1)}), bf16[4,4,768,128]{3,2,1,0:T(8,128)(2,1)S(1)}, u32[]{:S(2)}, u32[]{:S(2)}) async-start(bf16[4,4,768,128]{3,2,1,0:T(8,128)(2,1)} %broadcast_in_dim.12), calls=%async_computation.2 | async-start | bytes 6291456 | tf_op jit(solution)/shard_map/all_to_all | solution.py:50
  58.4 0.0 collective-permute-done
  58.4 3.7 %constant_dynamic-update-slice_fusion.2 = bf16[464,8192]{1,0:T(8,128)(2,1)} fusion(bf16[464,8192]{1,0:T(8,128)(2,1)} %constant_dynamic-update-slice_fusion.3, bf16[168,8192]{1,0:T(8,128)(2,1)} %collective-permute-done), kind=kLoop, calls=%fused_computation.6 | loop fusion | bytes 5505024
  62.1 2.3 %constant_dynamic-update-slice_fusion.1 = bf16[464,8192]{1,0:T(8,128)(2,1)} fusion(bf16[464,8192]{1,0:T(8,128)(2,1)} %constant_dynamic-update-slice_fusion.2, bf16[64,8192]{1,0:T(8,128)(2,1)} %param.16), kind=kLoop, calls=%fused_computation.5 | loop fusion | bytes 2097152
  64.4 0.0 copy-done.2
  64.4 1.0 constant_dynamic-update-slice_fusion.w_ref
  65.5 13.9 %all-to-all-done.2 = bf16[4,4,768,128]{3,2,1,0:T(8,128)(2,1)S(1)} async-done(((bf16[4,4,768,128]{3,2,1,0:T(8,128)(2,1)}), bf16[4,4,768,128]{3,2,1,0:T(8,128)(2,1)S(1)}, u32[]{:S(2)}, u32[]{:S(2)}) %all-to-all-start.2) | async-done | bytes 3145760 | tf_op jit(solution)/shard_map/all_to_all | solution.py:50
  79.4 7.9 %shard_map.109 = (f32[16,16,128]{2,1,0:T(8,128)S(1)}, f32[128,128]{1,0:T(8,128)S(1)}) custom-call(s32[1]{0:T(128)} %bitcast.core_ref, bf16[16,768,128]{2,1,0:T(8,128)(2,1)S(1)} %bitcast.25, bf16[16,768,128]{2,1,0:T(8,128)(2,1)S(1)} %bitcast.26, bf16[464,8192]{1,0:T(8,128)(2,1)} %constant_dynamic-update-slice_fusion.w_ref, ...), custom_call_target="tpu_custom_call" | custom-call | flops 1946157056 | bytes 12582912 | tf_op jit(solution)/shard_map/pallas_call | solution.py:127
  87.3 10.0 %all_to_all.30 = f32[16,16,128]{2,1,0:T(8,128)S(1)} all-to-all(f32[16,16,128]{2,1,0:T(8,128)S(1)} %get-tuple-element.7), channel_id=1, replica_groups={{0,2,4,6,8,10,12,14,16,18,20,22,24,26,28,30},{1,3,5,7,9,11,13,15,17,19,..., dimensions={0} | all-to-all | bytes 262144 | tf_op jit(solution)/shard_map/all_to_all | solution.py:50
  97.3 18.1 %all_to_all.31 = f32[16,16,128]{2,1,0:T(8,128)S(1)} all-to-all(f32[16,16,128]{2,1,0:T(8,128)S(1)} %broadcast_in_dim.13), channel_id=1, replica_groups={{0,32,64,96,128,160,192,224,256,288,320,352,384,416,448,480},{1,33,65,9..., dimensions={0} | all-to-all | bytes 262144 | tf_op jit(solution)/shard_map/all_to_all | solution.py:50
  115.5 0.7 broadcast_in_dim.14
  116.2 9.3 %all-to-all-start.5 = ((f32[32,16,128]{2,1,0:T(8,128)}), f32[32,16,128]{2,1,0:T(8,128)S(1)}, u32[]{:S(2)}, u32[]{:S(2)}) async-start(f32[32,16,128]{2,1,0:T(8,128)} %broadcast_in_dim.14), calls=%async_computation.5 | async-start | bytes 524288 | tf_op jit(solution)/shard_map/all_to_all | solution.py:50
  125.5 0.0 copy-done.3
  125.5 0.1 reshape.58
  125.6 0.1 pad.4
  125.7 1.9 %all-gather = f32[256,128]{1,0:T(8,128)S(1)} all-gather(f32[128,128]{1,0:T(8,128)S(1)} %get-tuple-element.8), channel_id=2, replica_groups={{0,1},{2,3},{4,5},{6,7},{8,9},{10,11},{12,13},{14,15},{16,17},{18,19},{..., dimensions={0}, use_global_device_ids=true | all-gather | bytes 196608 | tf_op jit(solution)/shard_map/all_gather | solution.py:231
  127.6 6.8 %all-to-all-done.5 = f32[32,16,128]{2,1,0:T(8,128)S(1)} async-done(((f32[32,16,128]{2,1,0:T(8,128)}), f32[32,16,128]{2,1,0:T(8,128)S(1)}, u32[]{:S(2)}, u32[]{:S(2)}) %all-to-all-start.5) | async-done | bytes 262176 | tf_op jit(solution)/shard_map/all_to_all | solution.py:50
  134.4 1.4 %shard_map.110 = f32[3,512,64]{2,1,0:T(8,128)S(1)} custom-call(f32[16,2,16,128]{3,2,1,0:T(8,128)S(1)} %bitcast.27, f32[2,128,128]{2,1,0:T(8,128)S(1)} %bitcast.28, s32[1,256]{1,0:T(1,128)S(1)} %bitcast.29), custom_call_target="tpu_custom_call" | custom-call | flops 301989888 | bytes 2097152 | tf_op jit(solution)/shard_map/pallas_call | solution.py:183
  135.8 1.0 reshape.60
  (12 shorter events, 0.1 us)
Async XLA Ops:
  0.0 31.9 %copy-start = (bf16[56,8192]{1,0:T(8,128)(2,1)S(1)}, bf16[56,8192]{1,0:T(8,128)(2,1)}, u32[]{:S(2)}) copy-start(bf16[56,8192]{1,0:T(8,128)(2,1)} %param.14) | copy-start | bytes 2752516
  0.0 43.7 %copy-start.1 = (bf16[56,8192]{1,0:T(8,128)(2,1)S(1)}, bf16[56,8192]{1,0:T(8,128)(2,1)}, u32[]{:S(2)}) copy-start(bf16[56,8192]{1,0:T(8,128)(2,1)} %param.15) | copy-start | bytes 2752516
  2.7 35.4 %all-to-all-start = ((bf16[32,24,128]{2,1,0:T(8,128)(2,1)}), bf16[32,24,128]{2,1,0:T(8,128)(2,1)S(1)}, u32[]{:S(2)}, u32[]{:S(2)}) async-start(bf16[32,24,128]{2,1,0:T(8,128)(2,1)} %bitcast.6), calls=%async_computation | async-start | bytes 393216 | tf_op jit(solution)/shard_map/all_to_all | solution.py:50
  23.0 35.4 %collective-permute-start = (bf16[168,8192]{1,0:T(8,128)(2,1)}, bf16[168,8192]{1,0:T(8,128)(2,1)}, u32[]{:S(2)}, u32[]{:S(2)}) collective-permute-start(bf16[168,8192]{1,0:T(8,128)(2,1)} %pad_maximum_fusion), channel_id=1, source_target_pairs={{0,1},{1,0},{2,3},{3,2},{4,5},{5,4},{6,7},{7,6},{8,9},{9,8},{10,11... | collective-permute-start | bytes 8257544 | tf_op jit(solution)/shard_map/ppermute | solution.py:225
  27.6 17.1 %collective-permute-start.1 = (bf16[3,64,56]{2,1,0:T(8,128)(2,1)S(1)}, bf16[3,64,56]{2,1,0:T(8,128)(2,1)S(1)}, u32[]{:S(2)}, u32[]{:S(2)}) collective-permute-start(bf16[3,64,56]{2,1,0:T(8,128)(2,1)S(1)} %pad_maximum_fusion.2), channel_id=1, source_target_pairs={{0,1},{1,0},{2,3},{3,2},{4,5},{5,4},{6,7},{7,6},{8,9},{9,8},{10,11... | collective-permute-start | bytes 64520 | tf_op jit(solution)/shard_map/ppermute | solution.py:228
  39.5 12.8 %all-to-all-start.1 = ((bf16[4,768,128]{2,1,0:T(8,128)(2,1)}), bf16[4,768,128]{2,1,0:T(8,128)(2,1)S(1)}, u32[]{:S(2)}, u32[]{:S(2)}) async-start(bf16[4,768,128]{2,1,0:T(8,128)(2,1)} %broadcast_in_dim.11), calls=%async_computation.1 | async-start | bytes 1572864 | tf_op jit(solution)/shard_map/all_to_all | solution.py:50
  54.7 24.7 %all-to-all-start.2 = ((bf16[4,4,768,128]{3,2,1,0:T(8,128)(2,1)}), bf16[4,4,768,128]{3,2,1,0:T(8,128)(2,1)S(1)}, u32[]{:S(2)}, u32[]{:S(2)}) async-start(bf16[4,4,768,128]{3,2,1,0:T(8,128)(2,1)} %broadcast_in_dim.12), calls=%async_computation.2 | async-start | bytes 6291456 | tf_op jit(solution)/shard_map/all_to_all | solution.py:50
  58.4 6.0 %copy-start.2 = (bf16[64,8192]{1,0:T(8,128)(2,1)S(1)}, bf16[64,8192]{1,0:T(8,128)(2,1)}, u32[]{:S(2)}) copy-start(bf16[64,8192]{1,0:T(8,128)(2,1)} %param.17) | copy-start | bytes 3145732
  79.4 46.2 %copy-start.3 = (s32[192]{0:T(256)S(1)}, s32[192]{0:T(256)}, u32[]{:S(2)}) copy-start(s32[192]{0:T(256)} %param.21) | copy-start | bytes 2308
  116.2 18.2 %all-to-all-start.5 = ((f32[32,16,128]{2,1,0:T(8,128)}), f32[32,16,128]{2,1,0:T(8,128)S(1)}, u32[]{:S(2)}, u32[]{:S(2)}) async-start(f32[32,16,128]{2,1,0:T(8,128)} %broadcast_in_dim.14), calls=%async_computation.5 | async-start | bytes 524288 | tf_op jit(solution)/shard_map/all_to_all | solution.py:50

commit v2 on v1

v2 whole, which is shorter than its diff:
```python
import jax
import jax.numpy as jnp
from jax import lax
from jax.experimental import pallas as pl
from jax.experimental.pallas import tpu as pltpu
from jax.sharding import PartitionSpec as P

DOCS = 8
BOTH = ("dp", "mp")
NZ, NXL, NY, NXH, NC = 16, 2, 4, 2, 2
NX = NXL * NXH
PLANE = NX * NY
LOW = 32
HALF = 96
MIB = 1 << 20


def device(z, xl, y, xh, c):
    return (((z * NXL + xl) * NY + y) * NXH + xh) * NC + c


def along_x(z, y, c):
    return [device(z, xl, y, xh, c) for xl in range(NXL) for xh in range(NXH)]


def along_y(z, xl, xh, c):
    return [device(z, xl, y, xh, c) for y in range(NY)]


def x_groups(c):
    return [along_x(z, y, c) for z in range(NZ) for y in range(NY)]


def y_groups(c):
    return [along_y(z, xl, xh, c) for z in range(NZ) for xl in range(NXL) for xh in range(NXH)]


SITES = [(xl, y, xh) for xl in range(NXL) for y in range(NY) for xh in range(NXH)]
COLUMN_GROUPS = [[device(z, *s, c) for z in range(NZ) for c in range(NC)] for s in SITES]
Z_GROUPS = [[device(z, *s, c) for z in range(NZ)] for s in SITES for c in range(NC)]
FIRST_GROUPS = x_groups(0) + y_groups(1)
SECOND_GROUPS = y_groups(0) + x_groups(1)
PLANE_GROUPS = [[device(z, *s, c) for s in SITES] for z in range(NZ) for c in range(NC)]
LAYER_GROUPS = [[device(z, *s, c) for s in SITES for c in range(NC)] for z in range(NZ)]
PAIRS = [[2 * i, 2 * i + 1] for i in range(NZ * PLANE)]
SWAP = [(i, i ^ 1) for i in range(NZ * PLANE * NC)]


def ring(shift):
    pairs = []
    for z in range(NZ):
        for xl, y, xh in SITES:
            pairs.append((device(z, xl, y, xh, 0), device(z, xl, (y + shift) % NY, xh, 0)))
            x = (xh * NXL + xl + shift) % NX
            pairs.append((device(z, xl, y, xh, 1), device(z, x % NXL, y, x // NXL, 1)))
    return pairs


def exchange(blocks, groups):
    return lax.all_to_all(blocks, BOTH, 0, 0, axis_index_groups=groups)


def spread(block, groups):
    number = len(groups[0])
    return exchange(jnp.broadcast_to(block[None], (number,) + block.shape), groups)


def columns(a, b):
    return lax.dot_general(a, b, (((1,), (0,)), ((), ())), preferred_element_type=jnp.float32)


SHIFTS = (0, 2, 1, 3)
SLABS = 8
ROWS = 192


def block_kernel(dest_ref, *refs):
    wide_refs, rest_refs = refs[0:4], refs[4:8]
    own_ref, other_ref, in_ref, out_ref, own_low_ref, other_low_ref = refs[8:14]
    f_ref, h_ref, x_ref, acc_ref, s_ref = refs[14:]
    step = pl.program_id(0)
    lane16 = lax.broadcasted_iota(jnp.int32, (16, 128), 1)
    first = (lane16 < 64).astype(jnp.float32).astype(jnp.bfloat16)
    second = (lane16 >= 64).astype(jnp.float32).astype(jnp.bfloat16)
    for k in range(4):
        for j in range(4):
            place = dest_ref[k * 4 + j]
            for slab in range(SLABS):
                base = pl.multiple_of(slab * 512 + place, 32)
                x_ref[pl.ds(base, 32), 0:128] = wide_refs[k][j, slab * 32 : slab * 32 + 32, :]
                tile = rest_refs[k][j, slab * 16 : slab * 16 + 16, :]
                x_ref[pl.ds(base, 16), 128:256] = tile * first
                x_ref[pl.ds(pl.multiple_of(base + 16, 16), 16), 128:256] = tile * second
    left = jnp.concatenate([own_ref[...], other_ref[...], in_ref[...], out_ref[...]], axis=0)
    product = columns(left, x_ref[...])

    @pl.when(step == 0)
    def _():
        acc_ref[...] = product

    @pl.when(step > 0)
    def _():
        acc_ref[...] += product

    @pl.when(step == pl.num_programs(0) - 1)
    def _():
        def rows(start, size, lanes):
            return acc_ref[start : start + size, lanes * 128 : lanes * 128 + 128]

        def both(start):
            return jnp.concatenate([rows(start, 56, 0), rows(start + 192, 56, 0)], axis=0)

        def grads(ranges):
            low = jnp.concatenate([rows(*r, 0) for r in ranges], axis=0)
            high = jnp.concatenate([rows(*r, 1) for r in ranges], axis=0)
            lane = lax.broadcasted_iota(jnp.int32, low.shape, 1)
            return jnp.where(lane < 64, pltpu.roll(low, 32, 1), high + pltpu.roll(high, 64, 1))

        gate_sum, up_sum = both(0), both(64)
        hidden_grad = grads([(128, 56), (320, 56)])
        sigmoid_gate = jax.nn.sigmoid(gate_sum)
        silu_gate = gate_sum * sigmoid_gate
        hidden = (silu_gate * up_sum).astype(jnp.bfloat16)
        gate_grad = (
            hidden_grad * up_sum * sigmoid_gate * (1.0 + gate_sum * (1.0 - sigmoid_gate))
        ).astype(jnp.bfloat16)
        up_grad = (hidden_grad * silu_gate).astype(jnp.bfloat16)
        for n, factor in enumerate((gate_grad, up_grad, hidden)):
            start = n * 64 + 56
            projection = jnp.concatenate(
                [
                    ref[start : start + 8, m * 128 : m * 128 + 64].astype(jnp.float32)
                    for ref in (own_low_ref, other_low_ref)
                    for m in range(7)
                ],
                axis=0,
            ).astype(jnp.bfloat16)
            s_ref[n * 64 : n * 64 + 64] = lax.dot_general(
                projection,
                factor,
                (((0,), (0,)), ((), ())),
                preferred_element_type=jnp.float32,
            )
        for p in range(PLANE):
            for r in range(3):
                f_ref[p, r] = s_ref[p * 12 + r * 4 : p * 12 + r * 4 + 4, :]
        h_ref[0:64] = rows(384, 64, 0)
        h_ref[64:128] = grads([(448, 64)])


def block(dest, lines, own, other, input_proj, output_proj):
    steps = NZ // SLABS
    wide = pl.BlockSpec((4, 32 * SLABS, 128), lambda s: (0, s, 0))
    rest = pl.BlockSpec((4, 16 * SLABS, 128), lambda s: (0, 512 // (16 * SLABS) + s, 0))
    return pl.pallas_call(
        block_kernel,
        grid=(steps,),
        in_specs=[pl.BlockSpec(memory_space=pltpu.SMEM)]
        + [wide] * 4
        + [rest] * 4
        + [
            pl.BlockSpec((ROWS, 512 * SLABS), lambda s: (0, s)),
            pl.BlockSpec((ROWS, 512 * SLABS), lambda s: (0, s)),
            pl.BlockSpec((64, 512 * SLABS), lambda s: (0, s)),
            pl.BlockSpec((64, 512 * SLABS), lambda s: (0, s)),
            pl.BlockSpec((ROWS, 1024), lambda s: (0, 0)),
            pl.BlockSpec((ROWS, 1024), lambda s: (0, 0)),
        ],
        out_specs=[
            pl.BlockSpec((PLANE, 3, 4, 128), lambda s: (0, 0, 0, 0)),
            pl.BlockSpec((128, 128), lambda s: (0, 0)),
        ],
        out_shape=[
            jax.ShapeDtypeStruct((PLANE, 3, 4, 128), jnp.float32),
            jax.ShapeDtypeStruct((128, 128), jnp.float32),
        ],
        scratch_shapes=[
            pltpu.VMEM((512 * SLABS, 256), jnp.bfloat16),
            pltpu.VMEM((2 * ROWS + 128, 256), jnp.float32),
            pltpu.VMEM((192, 128), jnp.float32),
        ],
        compiler_params=pltpu.CompilerParams(vmem_limit_bytes=28 * MIB),
        cost_estimate=pl.CostEstimate(
            flops=2 * 512 * 8192 * 256, bytes_accessed=12 * MIB, transcendentals=112 * 128
        ),
    )(dest, *lines, *lines, own, other, input_proj, output_proj, own, other)


def stack_kernel(gate_ref, up_ref, down_ref, *refs):
    out_ref = refs[3]
    for n, ref in enumerate((gate_ref, up_ref, down_ref)):
        out_ref[n * 64 : n * 64 + 56, :] = ref[...]
        out_ref[n * 64 + 56 : n * 64 + 64, :] = jnp.zeros((8, out_ref.shape[1]), jnp.bfloat16)

    @pl.when(pl.program_id(0) == 0)
    def _():
        for n in range(3):
            for m in range(7):
                piece = refs[n][m * 8 : m * 8 + 8, :]
                out_ref[n * 64 + 56 : n * 64 + 64, m * 128 : m * 128 + 64] = piece


def stack(weights, projections):
    width = 2048
    weight = pl.BlockSpec((56, width), lambda s: (0, s))
    projection = pl.BlockSpec((56, 64), lambda s: (0, 0))
    return pl.pallas_call(
        stack_kernel,
        grid=(8192 // width,),
        in_specs=[weight] * 3 + [projection] * 3,
        out_specs=pl.BlockSpec((ROWS, width), lambda s: (0, s)),
        out_shape=jax.ShapeDtypeStruct((ROWS, 8192), jnp.bfloat16),
        cost_estimate=pl.CostEstimate(flops=0, bytes_accessed=6 * MIB, transcendentals=0),
    )(*weights, *projections)


def pack_kernel(t_ref, g_ref, out_ref):
    t, g = t_ref[...].astype(jnp.float32), g_ref[...].astype(jnp.float32)
    for c in range(NC):
        start = c * HALF
        mine = jnp.concatenate([g[:, start : start + LOW], t[:, start : start + HALF]], axis=1)
        rest = g[:, start + LOW : start + HALF]
        rest = jnp.concatenate([rest[0:8], rest[8:16]], axis=1)
        packed = jnp.concatenate([mine, rest], axis=0).astype(jnp.bfloat16)
        for z in range(NZ):
            out_ref[z * NC + c] = packed


def pack(tokens, out_grad):
    return pl.pallas_call(
        pack_kernel,
        out_shape=jax.ShapeDtypeStruct((NZ * NC, 24, 128), jnp.bfloat16),
        cost_estimate=pl.CostEstimate(flops=0, bytes_accessed=1 << 18, transcendentals=0),
    )(tokens, out_grad)


def unpack_kernel(column_ref, out_ref):
    left = lax.broadcasted_iota(jnp.int32, (8, 128), 1) < 64
    for z in range(NZ):
        halves = []
        for c in range(NC):
            block = column_ref[z * NC + c].astype(jnp.float32)
            halves.append(block[16:24])
            for n in range(4):
                row = (z * NC + c) * 16
                out_ref[n, row : row + 16, :] = block[0:16].astype(jnp.bfloat16)
        top = jnp.where(left, halves[0], pltpu.roll(halves[1], 64, 1))
        low = jnp.where(left, pltpu.roll(halves[0], 64, 1), halves[1])
        rest = jnp.concatenate([top, low], axis=0).astype(jnp.bfloat16)
        for n in range(4):
            out_ref[n, 512 + z * 16 : 528 + z * 16, :] = rest


def unpack(column):
    return pl.pallas_call(
        unpack_kernel,
        out_shape=jax.ShapeDtypeStruct((4, 768, 128), jnp.bfloat16),
        cost_estimate=pl.CostEstimate(flops=0, bytes_accessed=MIB, transcendentals=0),
    )(column)


def outer_kernel(f_ref, h_ref, ids_ref, out_ref, s_ref):
    for p in range(PLANE):
        for c in range(NC):
            for r in range(3):
                row = p * 12 + r * 4
                s_ref[row : row + 4, c * 128 : c * 128 + 128] = f_ref[p, c, r]
    known = jnp.concatenate([h_ref[0], h_ref[1]], axis=1)
    doc = lax.broadcasted_iota(jnp.int32, (DOCS, NC * 128), 0)
    inside = (ids_ref[...] == doc)[None]
    sides = (
        (s_ref[0:64, :], known[0:64]),
        (s_ref[64:128, :], known[0:64]),
        (known[64:128], s_ref[128:192, :]),
    )
    for k, (left, right) in enumerate(sides):
        stacked = jnp.where(inside, left[:, None, :], 0.0).reshape(64 * DOCS, NC * 128)
        blocks = lax.dot_general(
            stacked,
            right,
            (((1,), (1,)), ((), ())),
            precision=lax.Precision.HIGHEST,
            preferred_element_type=jnp.float32,
        )
        for i in range(0, 64, 2):
            pair = [blocks[(i + n) * DOCS : (i + n + 1) * DOCS] for n in range(2)]
            out_ref[k, :, i * 64 : i * 64 + 128] = jnp.concatenate(pair, axis=1)


def outer(factors, known, ids):
    return pl.pallas_call(
        outer_kernel,
        out_shape=jax.ShapeDtypeStruct((3, DOCS, 4096), jnp.float32),
        scratch_shapes=[pltpu.VMEM((192, 256), jnp.float32)],
        compiler_params=pltpu.CompilerParams(vmem_limit_bytes=16 * MIB),
        cost_estimate=pl.CostEstimate(
            flops=2 * 3 * 512 * 256 * 64 * 6, bytes_accessed=2 * MIB, transcendentals=0
        ),
    )(factors, known, ids)


def local(
    tokens,
    out_grad,
    gate_weight,
    up_weight,
    down_weight,
    input_proj,
    output_proj,
    gate_proj,
    up_proj,
    hidden_proj,
    doc_ids,
):
    me = lax.axis_index("dp") * 16 + lax.axis_index("mp")
    core, x, y = me % NC, me // 2 % NXH * NXL + me // 16 % NXL, me // 4 % NY
    column = exchange(pack(tokens.T, out_grad.T), COLUMN_GROUPS)
    line = exchange(unpack(column), FIRST_GROUPS)
    lines = [line] + [lax.ppermute(line, BOTH, ring(shift)) for shift in SHIFTS[1:]]
    dest = []
    for shift in SHIFTS:
        from_y, from_x = (y - shift) % NY, (x - shift) % NX
        for j in range(4):
            even = j // NXH * 8 + from_y * 2 + j % NXH
            odd = from_x % NXL * 8 + j * 2 + from_x // NXL
            dest.append(jnp.where(core == 0, even, odd) * 32)
    dest = jnp.stack(dest).astype(jnp.int32)

    own = stack((gate_weight, up_weight, down_weight), (gate_proj, up_proj, hidden_proj))
    other = lax.ppermute(own, BOTH, SWAP)

    factors, known = block(dest, lines, own, other, input_proj, output_proj)
    known = lax.all_gather(known, BOTH, axis=0, axis_index_groups=PAIRS)
    part = exchange(factors, PLANE_GROUPS).sum(0)
    part = spread(part, Z_GROUPS).sum(0)
    factors = spread(part, LAYER_GROUPS).reshape(PLANE, NC, 3, 4, 128)
    ids = jnp.pad(doc_ids.reshape(NC, HALF), ((0, 0), (LOW, 0)), constant_values=-1)
    return outer(factors, known, ids.reshape(1, NC * 128))


def solution(mesh):
    return jax.shard_map(
        local,
        mesh=mesh,
        in_specs=(
            P(None, BOTH),
            P(None, BOTH),
            P(BOTH, None),
            P(BOTH, None),
            P(BOTH, None),
            P(),
            P(),
            P(BOTH, None),
            P(BOTH, None),
            P(BOTH, None),
            P(),
        ),
        out_specs=P(),
        check_vma=False,
    )
```

time: 138 us -> 137 us (level)
  blocking collectives: 30 us -> 68.7 us
  local copies, waits for them, and re-layouts: 22 us -> 3.43 us
  waiting for transfers between devices: 33.3 us -> 18.2 us
  starting transfers between devices: 38.3 us -> 30 us
  Pallas kernels: 9.33 us -> 15.6 us
  other arithmetic: 3.78 us -> 0.07 us
    all_to_all x2 -> x4, blocking collectives: 28.1 us -> 66.8 us  [exchange(): return lax.all_to_all(blocks, BOTH, 0, 0, axis_index_groups=groups)]
    all_to_all x4 -> x1, waiting for transfers between devices: 33.3 us -> 6.15 us  [exchange(): return lax.all_to_all(blocks, BOTH, 0, 0, axis_index_groups=groups)]
    all_to_all x4 -> x1, starting transfers between devices: 34 us -> 9.91 us  [exchange(): return lax.all_to_all(blocks, BOTH, 0, 0, axis_index_groups=groups)]
    ppermute x2 -> x4, starting transfers between devices: 4.32 us -> 20.1 us  [the longest x3 11.1 us: local(): lax.ppermute(line, BOTH, ring(shift))]
    ppermute x2 -> x4, waiting for transfers between devices: 0.01 us -> 12 us  [the longest x3 12 us: local(): lax.ppermute(line, BOTH, ring(shift))]
    unnamed x16 -> x8, local copies, waits for them, and re-layouts: 12.7 us -> 2.46 us
    pallas_call x1 -> x4, Pallas kernels: 1.41 us -> 9.9 us  [the longest x1 4.24 us: stack(): pl.pallas_call(stack_kernel, grid=(8192 // width,), in_specs=[weight] * 3...]
    concatenate x3 -> x0, other arithmetic: 3.63 us -> none  [the longest x1 3.53 us: local(): own = jnp.concatenate([gate_weight, up_weight, down_weight], axis=0)]
  transfers between devices with their start and end apart: 6 -> 5, of which waited for: 4 -> 4; matrix products, arithmetic and copies ran while one was open for 16% -> 0% of each run, Pallas kernels for 0% -> 2%
where the time goes in v2:
time: 137 us; the launch traced here: 136 us
  blocking collectives  68.7 us (50%)
  starting transfers between devices  30 us (22%)
  waiting for transfers between devices  18.2 us (13%)
  Pallas kernels  15.6 us (11%)
  local copies, waits for them, and re-layouts  3.43 us (3%)
    all_to_all x4, blocking collectives, exchange(): return lax.all_to_all(blocks, BOTH, 0, 0, axis_index_groups=groups)  66.8 us
    ppermute x3, waiting for transfers between devices, local(): lax.ppermute(line, BOTH, ring(shift))  12 us
    ppermute x3, starting transfers between devices, local(): lax.ppermute(line, BOTH, ring(shift))  11.1 us
    all_to_all x1, starting transfers between devices, exchange(): return lax.all_to_all(blocks, BOTH, 0, 0, axis_index_groups=groups)  9.91 us
    ppermute x1, starting transfers between devices, local(): other = lax.ppermute(own, BOTH, SWAP)  9.04 us
    all_to_all x1, waiting for transfers between devices, exchange(): return lax.all_to_all(blocks, BOTH, 0, 0, axis_index_groups=groups)  6.15 us
    pallas_call x1, Pallas kernels, block(): pl.pallas_call(block_kernel, grid=(steps,), in_specs=[pl.BlockSpec(memory...  5.73 us
    pallas_call x1, Pallas kernels, stack(): pl.pallas_call(stack_kernel, grid=(8192 // width,), in_specs=[weight] * 3...  4.24 us
  transfers between devices with their start and end apart: 5, of which 4 were waited for; matrix products, arithmetic and copies ran while one was open for 0% of the time, Pallas kernels for 2%

profile of v2, /device:TPU:1, one launch (start us, length us, event | category | flops | bytes accessed | tf_op | source)
XLA Modules:
  0.0 136.5 jit_solution(3929710924874126346)
XLA Ops:
  0.0 4.2 %shard_map.111.refs_8_.refs_12_ = bf16[192,8192]{1,0:T(8,128)(2,1)} custom-call(bf16[56,8192]{1,0:T(8,128)(2,1)} %gate_ref.1, bf16[56,8192]{1,0:T(8,128)(2,1)} %up_ref.1, bf16[56,8192]{1,0:T(8,128)(2,1)} %down_ref.1, bf16[56,64]{1,0:T(8,128)(2,1)} %refs_0_.1, bf16[56,64]{1,0:T(8,128)(2,1)} %refs_1_.1, bf16[56,64]{1,0:T(8,128)(2,1)} %refs_2_.1), custom_call_target="tpu_custom_call" | custom-call | bytes 6291456 | tf_op jit(solution)/shard_map/pallas_call | solution.py:207
  4.2 0.0 copy-start
  4.2 9.0 %collective-permute-start.3 = (bf16[192,8192]{1,0:T(8,128)(2,1)}, bf16[192,8192]{1,0:T(8,128)(2,1)}, u32[]{:S(2)}, u32[]{:S(2)}) collective-permute-start(bf16[192,8192]{1,0:T(8,128)(2,1)} %shard_map.111.refs_8_.refs_12_), channel_id=1, source_target_pairs={{0,1},{1,0},{2,3},{3,2},{4,5},{5,4},{6,7},{7,6},{8,9},{9,8},{10,11... | collective-permute-start | bytes 9437192 | tf_op jit(solution)/shard_map/ppermute | solution.py:330
  13.3 1.5 %shard_map.109 = bf16[32,24,128]{2,1,0:T(8,128)(2,1)} custom-call(bf16[16,192]{1,0:T(8,128)(2,1)} %bitcast.24, bf16[16,192]{1,0:T(8,128)(2,1)} %bitcast.25), custom_call_target="tpu_custom_call" | custom-call | bytes 262144 | tf_op jit(solution)/shard_map/pallas_call | solution.py:230
  14.8 28.7 %all_to_all.25.column_ref = bf16[32,24,128]{2,1,0:T(8,128)(2,1)} all-to-all(bf16[32,24,128]{2,1,0:T(8,128)(2,1)} %shard_map.109), channel_id=1, replica_groups={{0,1,32,33,64,65,96,97,128,129,160,161,192,193,224,225,256,257,288,289,..., dimensions={0} | all-to-all | bytes 393216 | tf_op jit(solution)/shard_map/all_to_all | solution.py:60
  43.5 1.9 %shard_map.110 = bf16[4,768,128]{2,1,0:T(8,128)(2,1)} custom-call(bf16[32,24,128]{2,1,0:T(8,128)(2,1)} %all_to_all.25.column_ref), custom_call_target="tpu_custom_call" | custom-call | bytes 1048576 | tf_op jit(solution)/shard_map/pallas_call | solution.py:255
  45.4 12.7 %all_to_all.26.refs_0_.refs_4_ = bf16[4,768,128]{2,1,0:T(8,128)(2,1)} all-to-all(bf16[4,768,128]{2,1,0:T(8,128)(2,1)} %shard_map.110), channel_id=1, replica_groups={{0,2,16,18},{4,6,20,22},{8,10,24,26},{12,14,28,30},{32,34,48,50},{36,38..., dimensions={0} | all-to-all | bytes 1572864 | tf_op jit(solution)/shard_map/all_to_all | solution.py:60
  58.0 4.6 %collective-permute-start = (bf16[4,768,128]{2,1,0:T(8,128)(2,1)}, bf16[4,768,128]{2,1,0:T(8,128)(2,1)}, u32[]{:S(2)}, u32[]{:S(2)}) collective-permute-start(bf16[4,768,128]{2,1,0:T(8,128)(2,1)} %all_to_all.26.refs_0_.refs_4_), channel_id=1, source_target_pairs={{0,8},{1,3},{2,10},{3,1},{4,12},{5,7},{6,14},{7,5},{8,0},{9,11},{1... | collective-permute-start | bytes 2359304 | tf_op jit(solution)/shard_map/ppermute | solution.py:319
  62.6 2.5 %collective-permute-start.1 = (bf16[4,768,128]{2,1,0:T(8,128)(2,1)}, bf16[4,768,128]{2,1,0:T(8,128)(2,1)}, u32[]{:S(2)}, u32[]{:S(2)}) collective-permute-start(bf16[4,768,128]{2,1,0:T(8,128)(2,1)} %all_to_all.26.refs_0_.refs_4_), channel_id=1, source_target_pairs={{0,4},{1,17},{2,6},{3,19},{4,8},{5,21},{6,10},{7,23},{8,12},{9,25}... | collective-permute-start | bytes 2359304 | tf_op jit(solution)/shard_map/ppermute | solution.py:319
  65.2 4.0 %collective-permute-start.2 = (bf16[4,768,128]{2,1,0:T(8,128)(2,1)}, bf16[4,768,128]{2,1,0:T(8,128)(2,1)}, u32[]{:S(2)}, u32[]{:S(2)}) collective-permute-start(bf16[4,768,128]{2,1,0:T(8,128)(2,1)} %all_to_all.26.refs_0_.refs_4_), channel_id=1, source_target_pairs={{0,12},{1,19},{2,14},{3,17},{4,0},{5,23},{6,2},{7,21},{8,4},{9,27}... | collective-permute-start | bytes 2359304 | tf_op jit(solution)/shard_map/ppermute | solution.py:319
  69.5 0.0 copy-start.3
  69.5 0.1 stack.67.dest_ref
  69.6 3.3 %collective-permute-done.refs_1_.refs_5_ = bf16[4,768,128]{2,1,0:T(8,128)(2,1)} collective-permute-done((bf16[4,768,128]{2,1,0:T(8,128)(2,1)}, bf16[4,768,128]{2,1,0:T(8,128)(2,1)}, u32[]{:S(2)}, u32[]{:S(2)}) %collective-permute-start) | collective-permute-done | bytes 786464 | tf_op jit(solution)/shard_map/ppermute | solution.py:319
  72.9 8.4 %collective-permute-done.1.refs_2_.refs_6_ = bf16[4,768,128]{2,1,0:T(8,128)(2,1)} collective-permute-done((bf16[4,768,128]{2,1,0:T(8,128)(2,1)}, bf16[4,768,128]{2,1,0:T(8,128)(2,1)}, u32[]{:S(2)}, u32[]{:S(2)}) %collective-permute-start.1) | collective-permute-done | bytes 786464 | tf_op jit(solution)/shard_map/ppermute | solution.py:319
  81.3 0.4 collective-permute-done.2.refs_3_.refs_7_
  81.7 0.0 collective-permute-done.3.refs_9_.refs_13_
  81.7 0.0 copy-done
  81.7 0.0 copy-start.1
  81.7 1.2 copy-done.1
  82.9 0.0 copy-start.2
  82.9 1.2 copy-done.2
  84.1 5.7 %shard_map.112 = (f32[16,3,4,128]{3,2,1,0:T(4,128)S(1)}, f32[128,128]{1,0:T(8,128)S(1)}) custom-call(s32[16]{0:T(128)S(1)} %stack.67.dest_ref, bf16[4,768,128]{2,1,0:T(8,128)(2,1)} %all_to_all.26.refs_0_.refs_4_, bf16[4,768,128]{2,1,0:T(8,128)(2,1)} %collective-permute-done.refs_1_.refs_5_, bf16[4,768,128]{2,1,0:T(8,128)(2,1)} %collective-permute-done.1.refs_2_.refs_6_, ...), custom_call_target="tpu_custom_call" | custom-call | flops 2147483648 | bytes 12582912 | tf_op jit(solution)/shard_map/pallas_call | solution.py:155
  89.9 11.0 %all_to_all.27 = f32[16,3,4,128]{3,2,1,0:T(4,128)S(1)} all-to-all(f32[16,3,4,128]{3,2,1,0:T(4,128)S(1)} %get-tuple-element.7), channel_id=1, replica_groups={{0,2,4,6,8,10,12,14,16,18,20,22,24,26,28,30},{1,3,5,7,9,11,13,15,17,19,..., dimensions={0} | all-to-all | bytes 196608 | tf_op jit(solution)/shard_map/all_to_all | solution.py:60
  100.9 14.4 %all_to_all.28 = f32[16,3,4,128]{3,2,1,0:T(4,128)S(1)} all-to-all(f32[16,3,4,128]{3,2,1,0:T(4,128)S(1)} %broadcast_in_dim.4), channel_id=1, replica_groups={{0,32,64,96,128,160,192,224,256,288,320,352,384,416,448,480},{1,33,65,9..., dimensions={0} | all-to-all | bytes 196608 | tf_op jit(solution)/shard_map/all_to_all | solution.py:60
  115.4 0.7 broadcast_in_dim.5
  116.1 9.9 %all-to-all-start.4 = ((f32[32,3,4,128]{3,2,1,0:T(4,128)}), f32[32,3,4,128]{3,2,1,0:T(4,128)S(1)}, u32[]{:S(2)}, u32[]{:S(2)}) async-start(f32[32,3,4,128]{3,2,1,0:T(4,128)} %broadcast_in_dim.5), calls=%async_computation.4 | async-start | bytes 393216 | tf_op jit(solution)/shard_map/all_to_all | solution.py:60
  126.0 0.0 copy-done.3
  126.0 0.1 reshape.12
  126.1 0.1 pad.4
  126.2 1.9 %all-gather = f32[256,128]{1,0:T(8,128)S(1)} all-gather(f32[128,128]{1,0:T(8,128)S(1)} %get-tuple-element.8), channel_id=2, replica_groups={{0,1},{2,3},{4,5},{6,7},{8,9},{10,11},{12,13},{14,15},{16,17},{18,19},{..., dimensions={0}, use_global_device_ids=true | all-gather | bytes 196608 | tf_op jit(solution)/shard_map/all_gather | solution.py:333
  128.1 6.1 %all-to-all-done.4 = f32[32,3,4,128]{3,2,1,0:T(4,128)S(1)} async-done(((f32[32,3,4,128]{3,2,1,0:T(4,128)}), f32[32,3,4,128]{3,2,1,0:T(4,128)S(1)}, u32[]{:S(2)}, u32[]{:S(2)}) %all-to-all-start.4) | async-done | bytes 196640 | tf_op jit(solution)/shard_map/all_to_all | solution.py:60
  134.2 2.3 %shard_map.113 = f32[3,8,4096]{2,1,0:T(8,128)} custom-call(f32[16,2,3,4,128]{4,3,2,1,0:T(4,128)S(1)} %bitcast.21, f32[2,128,128]{2,1,0:T(8,128)S(1)} %bitcast.22, s32[1,256]{1,0:T(1,128)S(1)} %bitcast.23), custom_call_target="tpu_custom_call" | custom-call | flops 301989888 | bytes 2097152 | tf_op jit(solution)/shard_map/pallas_call | solution.py:291
  (3 shorter events, 0.1 us)
Async XLA Ops:
  4.2 77.4 %copy-start = (bf16[192,8192]{1,0:T(8,128)(2,1)S(1)}, bf16[192,8192]{1,0:T(8,128)(2,1)}, u32[]{:S(2)}) copy-start(bf16[192,8192]{1,0:T(8,128)(2,1)} %shard_map.111.refs_8_.refs_12_) | copy-start | bytes 9437188
  4.2 77.4 %collective-permute-start.3 = (bf16[192,8192]{1,0:T(8,128)(2,1)}, bf16[192,8192]{1,0:T(8,128)(2,1)}, u32[]{:S(2)}, u32[]{:S(2)}) collective-permute-start(bf16[192,8192]{1,0:T(8,128)(2,1)} %shard_map.111.refs_8_.refs_12_), channel_id=1, source_target_pairs={{0,1},{1,0},{2,3},{3,2},{4,5},{5,4},{6,7},{7,6},{8,9},{9,8},{10,11... | collective-permute-start | bytes 9437192 | tf_op jit(solution)/shard_map/ppermute | solution.py:330
  58.0 14.9 %collective-permute-start = (bf16[4,768,128]{2,1,0:T(8,128)(2,1)}, bf16[4,768,128]{2,1,0:T(8,128)(2,1)}, u32[]{:S(2)}, u32[]{:S(2)}) collective-permute-start(bf16[4,768,128]{2,1,0:T(8,128)(2,1)} %all_to_all.26.refs_0_.refs_4_), channel_id=1, source_target_pairs={{0,8},{1,3},{2,10},{3,1},{4,12},{5,7},{6,14},{7,5},{8,0},{9,11},{1... | collective-permute-start | bytes 2359304 | tf_op jit(solution)/shard_map/ppermute | solution.py:319
  62.6 18.7 %collective-permute-start.1 = (bf16[4,768,128]{2,1,0:T(8,128)(2,1)}, bf16[4,768,128]{2,1,0:T(8,128)(2,1)}, u32[]{:S(2)}, u32[]{:S(2)}) collective-permute-start(bf16[4,768,128]{2,1,0:T(8,128)(2,1)} %all_to_all.26.refs_0_.refs_4_), channel_id=1, source_target_pairs={{0,4},{1,17},{2,6},{3,19},{4,8},{5,21},{6,10},{7,23},{8,12},{9,25}... | collective-permute-start | bytes 2359304 | tf_op jit(solution)/shard_map/ppermute | solution.py:319
  65.2 16.5 %collective-permute-start.2 = (bf16[4,768,128]{2,1,0:T(8,128)(2,1)}, bf16[4,768,128]{2,1,0:T(8,128)(2,1)}, u32[]{:S(2)}, u32[]{:S(2)}) collective-permute-start(bf16[4,768,128]{2,1,0:T(8,128)(2,1)} %all_to_all.26.refs_0_.refs_4_), channel_id=1, source_target_pairs={{0,12},{1,19},{2,14},{3,17},{4,0},{5,23},{6,2},{7,21},{8,4},{9,27}... | collective-permute-start | bytes 2359304 | tf_op jit(solution)/shard_map/ppermute | solution.py:319
  69.5 56.5 %copy-start.3 = (s32[192]{0:T(256)S(1)}, s32[192]{0:T(256)}, u32[]{:S(2)}) copy-start(s32[192]{0:T(256)} %param.21) | copy-start | bytes 2308
  81.7 1.2 copy-start.1
  82.9 1.2 copy-start.2
  116.1 18.1 %all-to-all-start.4 = ((f32[32,3,4,128]{3,2,1,0:T(4,128)}), f32[32,3,4,128]{3,2,1,0:T(4,128)S(1)}, u32[]{:S(2)}, u32[]{:S(2)}) async-start(f32[32,3,4,128]{3,2,1,0:T(4,128)} %broadcast_in_dim.5), calls=%async_computation.4 | async-start | bytes 393216 | tf_op jit(solution)/shard_map/all_to_all | solution.py:60

commit v3 on v2

v3 whole, which is shorter than its diff:
```python
import jax
import jax.numpy as jnp
from jax import lax
from jax.experimental import pallas as pl
from jax.experimental.pallas import tpu as pltpu
from jax.sharding import PartitionSpec as P

DOCS = 8
BOTH = ("dp", "mp")
NZ, NXL, NY, NXH, NC = 16, 2, 4, 2, 2
NX = NXL * NXH
PLANE = NX * NY
LOW = 32
HALF = 96
MIB = 1 << 20


def device(z, xl, y, xh, c):
    return (((z * NXL + xl) * NY + y) * NXH + xh) * NC + c


def along_x(z, y, c):
    return [device(z, xl, y, xh, c) for xl in range(NXL) for xh in range(NXH)]


def along_y(z, xl, xh, c):
    return [device(z, xl, y, xh, c) for y in range(NY)]


def x_groups(c):
    return [along_x(z, y, c) for z in range(NZ) for y in range(NY)]


def y_groups(c):
    return [along_y(z, xl, xh, c) for z in range(NZ) for xl in range(NXL) for xh in range(NXH)]


SITES = [(xl, y, xh) for xl in range(NXL) for y in range(NY) for xh in range(NXH)]
COLUMN_GROUPS = [[device(z, *s, c) for z in range(NZ) for c in range(NC)] for s in SITES]
Z_GROUPS = [[device(z, *s, c) for z in range(NZ)] for s in SITES for c in range(NC)]
FIRST_GROUPS = x_groups(0) + y_groups(1)
SECOND_GROUPS = y_groups(0) + x_groups(1)
PLANE_GROUPS = [[device(z, *s, c) for s in SITES] for z in range(NZ) for c in range(NC)]
LAYER_GROUPS = [[device(z, *s, c) for s in SITES for c in range(NC)] for z in range(NZ)]
PAIRS = [[2 * i, 2 * i + 1] for i in range(NZ * PLANE)]
SWAP = [(i, i ^ 1) for i in range(NZ * PLANE * NC)]


def ring(shift):
    pairs = []
    for z in range(NZ):
        for xl, y, xh in SITES:
            pairs.append((device(z, xl, y, xh, 0), device(z, xl, (y + shift) % NY, xh, 0)))
            x = (xh * NXL + xl + shift) % NX
            pairs.append((device(z, xl, y, xh, 1), device(z, x % NXL, y, x // NXL, 1)))
    return pairs


def exchange(blocks, groups):
    return lax.all_to_all(blocks, BOTH, 0, 0, axis_index_groups=groups)


def spread(block, groups):
    number = len(groups[0])
    return exchange(jnp.broadcast_to(block[None], (number,) + block.shape), groups)


def columns(a, b):
    return lax.dot_general(a, b, (((1,), (0,)), ((), ())), preferred_element_type=jnp.float32)


SHIFTS = (0, 2, 1, 3)
ROWS = 192
ALL_ROWS = 2 * ROWS + 2 * 64
GROUPS = 4
SLABS = NZ // GROUPS


def block_kernel(dest_ref, *refs):
    lines, w_ref, f_ref, h_ref, x_ref, acc_ref, s_ref = refs[0:4], *refs[4:]
    lane16 = lax.broadcasted_iota(jnp.int32, (16, 128), 1)
    first = (lane16 < 64).astype(jnp.float32).astype(jnp.bfloat16)
    second = (lane16 >= 64).astype(jnp.float32).astype(jnp.bfloat16)
    for group in range(GROUPS):
        for k in range(4):
            for j in range(4):
                place = dest_ref[k * 4 + j]
                for slab in range(group * SLABS, group * SLABS + SLABS):
                    base = pl.multiple_of(slab * 512 + place, 32)
                    x_ref[pl.ds(base, 32), 0:128] = lines[k][j, slab * 32 : slab * 32 + 32, :]
                    tile = lines[k][j, 512 + slab * 16 : 528 + slab * 16, :]
                    x_ref[pl.ds(base, 16), 128:256] = tile * first
                    x_ref[pl.ds(pl.multiple_of(base + 16, 16), 16), 128:256] = tile * second
        span = slice(group * SLABS * 512, (group + 1) * SLABS * 512)
        product = columns(w_ref[:, span], x_ref[span, :])
        if group == 0:
            acc_ref[...] = product
        else:
            acc_ref[...] += product

    def rows(start, size, lanes):
        return acc_ref[start : start + size, lanes * 128 : lanes * 128 + 128]

    def both(start):
        return jnp.concatenate([rows(start, 56, 0), rows(start + 192, 56, 0)], axis=0)

    def grads(ranges):
        low = jnp.concatenate([rows(*r, 0) for r in ranges], axis=0)
        high = jnp.concatenate([rows(*r, 1) for r in ranges], axis=0)
        lane = lax.broadcasted_iota(jnp.int32, low.shape, 1)
        return jnp.where(lane < 64, pltpu.roll(low, 32, 1), high + pltpu.roll(high, 64, 1))

    gate_sum, up_sum = both(0), both(64)
    hidden_grad = grads([(128, 56), (320, 56)])
    sigmoid_gate = jax.nn.sigmoid(gate_sum)
    silu_gate = gate_sum * sigmoid_gate
    hidden = (silu_gate * up_sum).astype(jnp.bfloat16)
    gate_grad = (
        hidden_grad * up_sum * sigmoid_gate * (1.0 + gate_sum * (1.0 - sigmoid_gate))
    ).astype(jnp.bfloat16)
    up_grad = (hidden_grad * silu_gate).astype(jnp.bfloat16)
    for n, factor in enumerate((gate_grad, up_grad, hidden)):
        start = n * 64 + 56
        projection = jnp.concatenate(
            [
                w_ref[base + start : base + start + 8, m * 128 : m * 128 + 64].astype(jnp.float32)
                for base in (0, ROWS)
                for m in range(7)
            ],
            axis=0,
        ).astype(jnp.bfloat16)
        s_ref[n * 64 : n * 64 + 64] = lax.dot_general(
            projection,
            factor,
            (((0,), (0,)), ((), ())),
            preferred_element_type=jnp.float32,
        )
    for p in range(PLANE):
        for r in range(3):
            f_ref[p, r] = s_ref[p * 12 + r * 4 : p * 12 + r * 4 + 4, :]
    h_ref[0:64] = rows(384, 64, 0)
    h_ref[64:128] = grads([(448, 64)])


def block(dest, lines, weights):
    inside = pl.BlockSpec(memory_space=pltpu.VMEM)
    return pl.pallas_call(
        block_kernel,
        in_specs=[pl.BlockSpec(memory_space=pltpu.SMEM)] + [inside] * 5,
        out_specs=[inside] * 2,
        out_shape=[
            jax.ShapeDtypeStruct((PLANE, 3, 4, 128), jnp.float32),
            jax.ShapeDtypeStruct((128, 128), jnp.float32),
        ],
        scratch_shapes=[
            pltpu.VMEM((8192, 256), jnp.bfloat16),
            pltpu.VMEM((ALL_ROWS, 256), jnp.float32),
            pltpu.VMEM((192, 128), jnp.float32),
        ],
        compiler_params=pltpu.CompilerParams(vmem_limit_bytes=24 * MIB),
        cost_estimate=pl.CostEstimate(
            flops=2 * ALL_ROWS * 8192 * 256, bytes_accessed=12 * MIB, transcendentals=112 * 128
        ),
    )(dest, *lines, weights)


def load_kernel(*refs):
    parts, w_ref, sems = refs[0:8], *refs[9:]
    copies = []
    for n, part in enumerate(parts):
        copies.append(pltpu.make_async_copy(part, w_ref.at[pl.ds(n * 64, 64)], sems.at[n]))
    for copy in copies:
        copy.start()
    for copy in copies:
        copy.wait()


def load(parts, after):
    return pl.pallas_call(
        load_kernel,
        in_specs=[pl.BlockSpec(memory_space=pl.ANY)] * 9,
        out_specs=pl.BlockSpec(memory_space=pltpu.VMEM),
        out_shape=pltpu.VMEM((ALL_ROWS, 8192), jnp.bfloat16),
        scratch_shapes=[pltpu.SemaphoreType.DMA((8,))],
        compiler_params=pltpu.CompilerParams(vmem_limit_bytes=16 * MIB),
        cost_estimate=pl.CostEstimate(flops=0, bytes_accessed=16 * MIB, transcendentals=0),
    )(*parts, after)


def stack_kernel(*refs):
    weights, projections, outs = refs[0:3], refs[3:6], refs[6:9]
    for weight, out in zip(weights, outs):
        out[0:56, :] = weight[...]
        out[56:64, :] = jnp.zeros((8, out.shape[1]), jnp.bfloat16)

    @pl.when(pl.program_id(0) == 0)
    def _():
        for projection, out in zip(projections, outs):
            for m in range(7):
                out[56:64, m * 128 : m * 128 + 64] = projection[m * 8 : m * 8 + 8, :]


def stack(weights, projections):
    width = 2048
    weight = pl.BlockSpec((56, width), lambda s: (0, s))
    projection = pl.BlockSpec((56, 64), lambda s: (0, 0))
    return pl.pallas_call(
        stack_kernel,
        grid=(8192 // width,),
        in_specs=[weight] * 3 + [projection] * 3,
        out_specs=[pl.BlockSpec((64, width), lambda s: (0, s))] * 3,
        out_shape=[jax.ShapeDtypeStruct((64, 8192), jnp.bfloat16)] * 3,
        cost_estimate=pl.CostEstimate(flops=0, bytes_accessed=6 * MIB, transcendentals=0),
    )(*weights, *projections)


def pack_kernel(t_ref, g_ref, out_ref):
    t, g = t_ref[...].astype(jnp.float32), g_ref[...].astype(jnp.float32)
    for c in range(NC):
        start = c * HALF
        mine = jnp.concatenate([g[:, start : start + LOW], t[:, start : start + HALF]], axis=1)
        rest = g[:, start + LOW : start + HALF]
        rest = jnp.concatenate([rest[0:8], rest[8:16]], axis=1)
        packed = jnp.concatenate([mine, rest], axis=0).astype(jnp.bfloat16)
        for z in range(NZ):
            out_ref[z * NC + c] = packed


def pack(tokens, out_grad):
    return pl.pallas_call(
        pack_kernel,
        out_shape=jax.ShapeDtypeStruct((NZ * NC, 24, 128), jnp.bfloat16),
        cost_estimate=pl.CostEstimate(flops=0, bytes_accessed=1 << 18, transcendentals=0),
    )(tokens, out_grad)


def outer_kernel(f_ref, h_ref, ids_ref, out_ref, s_ref):
    for p in range(PLANE):
        for c in range(NC):
            for r in range(3):
                row = p * 12 + r * 4
                s_ref[row : row + 4, c * 128 : c * 128 + 128] = f_ref[p, c, r]
    known = jnp.concatenate([h_ref[0], h_ref[1]], axis=1)
    doc = lax.broadcasted_iota(jnp.int32, (DOCS, NC * 128), 0)
    inside = (ids_ref[...] == doc)[None]
    sides = (
        (s_ref[0:64, :], known[0:64]),
        (s_ref[64:128, :], known[0:64]),
        (known[64:128], s_ref[128:192, :]),
    )
    for k, (left, right) in enumerate(sides):
        stacked = jnp.where(inside, left[:, None, :], 0.0).reshape(64 * DOCS, NC * 128)
        blocks = lax.dot_general(
            stacked,
            right,
            (((1,), (1,)), ((), ())),
            precision=lax.Precision.HIGHEST,
            preferred_element_type=jnp.float32,
        )
        for i in range(0, 64, 2):
            pair = [blocks[(i + n) * DOCS : (i + n + 1) * DOCS] for n in range(2)]
            out_ref[k, :, i * 64 : i * 64 + 128] = jnp.concatenate(pair, axis=1)


def outer(factors, known, ids):
    return pl.pallas_call(
        outer_kernel,
        out_shape=jax.ShapeDtypeStruct((3, DOCS, 4096), jnp.float32),
        scratch_shapes=[pltpu.VMEM((192, 256), jnp.float32)],
        compiler_params=pltpu.CompilerParams(vmem_limit_bytes=16 * MIB),
        cost_estimate=pl.CostEstimate(
            flops=2 * 3 * 512 * 256 * 64 * 6, bytes_accessed=2 * MIB, transcendentals=0
        ),
    )(factors, known, ids)


def local(
    tokens,
    out_grad,
    gate_weight,
    up_weight,
    down_weight,
    input_proj,
    output_proj,
    gate_proj,
    up_proj,
    hidden_proj,
    doc_ids,
):
    me = lax.axis_index("dp") * 16 + lax.axis_index("mp")
    core, x, y = me % NC, me // 2 % NXH * NXL + me // 16 % NXL, me // 4 % NY
    column = exchange(pack(tokens.T, out_grad.T), COLUMN_GROUPS)
    wide = column[:, :16, :].reshape(512, 128)
    rest = column[:, 16:, :].reshape(NZ, NC, 8, 2, 64)
    rest = rest.transpose(0, 3, 2, 1, 4).reshape(256, 128)
    column = jnp.concatenate([wide, rest], axis=0)
    own = stack((gate_weight, up_weight, down_weight), (gate_proj, up_proj, hidden_proj))
    other = [lax.ppermute(part, BOTH, SWAP) for part in own]
    line = spread(column, FIRST_GROUPS)
    lines = [line] + [lax.ppermute(line, BOTH, ring(shift)) for shift in SHIFTS[1:]]
    dest = []
    for shift in SHIFTS:
        from_y, from_x = (y - shift) % NY, (x - shift) % NX
        for j in range(4):
            even = j // NXH * 8 + from_y * 2 + j % NXH
            odd = from_x % NXL * 8 + j * 2 + from_x // NXL
            dest.append(jnp.where(core == 0, even, odd) * 32)
    dest = jnp.stack(dest).astype(jnp.int32)

    weights = load((*own, *other, input_proj, output_proj), line)
    factors, known = block(dest, lines, weights)
    known = lax.all_gather(known, BOTH, axis=0, axis_index_groups=PAIRS)
    part = exchange(factors, PLANE_GROUPS).sum(0)
    part = spread(part, Z_GROUPS).sum(0)
    factors = spread(part, LAYER_GROUPS).reshape(PLANE, NC, 3, 4, 128)
    ids = jnp.pad(doc_ids.reshape(NC, HALF), ((0, 0), (LOW, 0)), constant_values=-1)
    return outer(factors, known, ids.reshape(1, NC * 128))


def solution(mesh):
    return jax.shard_map(
        local,
        mesh=mesh,
        in_specs=(
            P(None, BOTH),
            P(None, BOTH),
            P(BOTH, None),
            P(BOTH, None),
            P(BOTH, None),
            P(),
            P(),
            P(BOTH, None),
            P(BOTH, None),
            P(BOTH, None),
            P(),
        ),
        out_specs=P(),
        check_vma=False,
    )
```

time: 137 us -> 127 us (0.927)
  blocking collectives: 68.7 us -> 27.4 us
  starting transfers between devices: 30 us -> 49.4 us
  waiting for transfers between devices: 18.2 us -> 27.2 us
  local copies, waits for them, and re-layouts: 3.43 us -> 6 us
    all_to_all x4 -> x2, blocking collectives: 66.8 us -> 25.5 us  [exchange(): return lax.all_to_all(blocks, BOTH, 0, 0, axis_index_groups=groups)]
    all_to_all x1 -> x3, starting transfers between devices: 9.91 us -> 30.9 us  [exchange(): return lax.all_to_all(blocks, BOTH, 0, 0, axis_index_groups=groups)]
    all_to_all x1 -> x3, waiting for transfers between devices: 6.15 us -> 21.4 us  [exchange(): return lax.all_to_all(blocks, BOTH, 0, 0, axis_index_groups=groups)]
    ppermute x3, waiting for transfers between devices: 12 us -> 5.81 us  [local(): lax.ppermute(line, BOTH, ring(shift))]
    ppermute x1 -> x3, starting transfers between devices: 9.04 us -> 7.71 us  [local(): other = [lax.ppermute(part, BOTH, SWAP) for part in own]]
    unnamed x8 -> x12, local copies, waits for them, and re-layouts: 2.46 us -> 3.68 us
  transfers between devices with their start and end apart: 5 -> 9, of which waited for: 4 -> 4; matrix products, arithmetic and copies ran while one was open for 0% -> 1% of each run, Pallas kernels for 2% -> 5%
where the time goes in v3:
time: 127 us; the launch traced here: 126 us
  starting transfers between devices  49.4 us (39%)
  blocking collectives  27.4 us (22%)
  waiting for transfers between devices  27.2 us (21%)
  Pallas kernels  15.1 us (12%)
  local copies, waits for them, and re-layouts  6 us (5%)
    all_to_all x3, starting transfers between devices, exchange(): return lax.all_to_all(blocks, BOTH, 0, 0, axis_index_groups=groups)  30.9 us
    all_to_all x2, blocking collectives, exchange(): return lax.all_to_all(blocks, BOTH, 0, 0, axis_index_groups=groups)  25.5 us
    all_to_all x3, waiting for transfers between devices, exchange(): return lax.all_to_all(blocks, BOTH, 0, 0, axis_index_groups=groups)  21.4 us
    ppermute x3, starting transfers between devices, local(): lax.ppermute(line, BOTH, ring(shift))  10.8 us
    ppermute x3, starting transfers between devices, local(): other = [lax.ppermute(part, BOTH, SWAP) for part in own]  7.71 us
    ppermute x3, waiting for transfers between devices, local(): lax.ppermute(line, BOTH, ring(shift))  5.81 us
    pallas_call x1, Pallas kernels, block(): pl.pallas_call(block_kernel, in_specs=[pl.BlockSpec(memory_space=pltpu.SM...  4.79 us
    pallas_call x1, Pallas kernels, stack(): pl.pallas_call(stack_kernel, grid=(8192 // width,), in_specs=[weight] * 3...  4.25 us
  transfers between devices with their start and end apart: 9, of which 4 were waited for; matrix products, arithmetic and copies ran while one was open for 1% of the time, Pallas kernels for 5%

profile of v3, /device:TPU:1, one launch (start us, length us, event | category | flops | bytes accessed | tf_op | source)
XLA Modules:
  0.0 125.9 jit_solution(8656563660429515122)
XLA Ops:
  0.0 0.0 copy-start
  0.0 0.0 copy-start.1
  0.0 1.6 %shard_map.109 = bf16[32,24,128]{2,1,0:T(8,128)(2,1)} custom-call(bf16[16,192]{1,0:T(8,128)(2,1)} %bitcast.28, bf16[16,192]{1,0:T(8,128)(2,1)} %bitcast.29), custom_call_target="tpu_custom_call" | custom-call | bytes 262144 | tf_op jit(solution)/shard_map/pallas_call | solution.py:230
  1.6 16.7 %all-to-all-start = ((bf16[32,24,128]{2,1,0:T(8,128)(2,1)}), bf16[32,24,128]{2,1,0:T(8,128)(2,1)S(1)}, u32[]{:S(2)}, u32[]{:S(2)}) async-start(bf16[32,24,128]{2,1,0:T(8,128)(2,1)} %shard_map.109), calls=%async_computation | async-start | bytes 393216 | tf_op jit(solution)/shard_map/all_to_all | solution.py:60
  18.4 4.3 %shard_map.110 = (bf16[64,8192]{1,0:T(8,128)(2,1)}, bf16[64,8192]{1,0:T(8,128)(2,1)}, bf16[64,8192]{1,0:T(8,128)(2,1)}) custom-call(bf16[56,8192]{1,0:T(8,128)(2,1)} %refs_0_.1, bf16[56,8192]{1,0:T(8,128)(2,1)} %refs_1_.1, bf16[56,8192]{1,0:T(8,128)(2,1)} %refs_2_.1, bf16[56,64]{1,0:T(8,128)(2,1)} %refs_3_.1, bf16[56,64]{1,0:T(8,128)(2,1)} %refs_4_.1, ...), custom_call_target="tpu_custom_call" | custom-call | bytes 6291456 | tf_op jit(solution)/shard_map/pallas_call | solution.py:207
  22.6 2.1 %collective-permute-start.3 = (bf16[64,8192]{1,0:T(8,128)(2,1)}, bf16[64,8192]{1,0:T(8,128)(2,1)}, u32[]{:S(2)}, u32[]{:S(2)}) collective-permute-start(bf16[64,8192]{1,0:T(8,128)(2,1)} %get-tuple-element.10.refs_0_), channel_id=1, source_target_pairs={{0,1},{1,0},{2,3},{3,2},{4,5},{5,4},{6,7},{7,6},{8,9},{9,8},{10,11... | collective-permute-start | bytes 3145736 | tf_op jit(solution)/shard_map/ppermute | solution.py:298
  24.8 12.2 %all-to-all-done = bf16[32,24,128]{2,1,0:T(8,128)(2,1)S(1)} async-done(((bf16[32,24,128]{2,1,0:T(8,128)(2,1)}), bf16[32,24,128]{2,1,0:T(8,128)(2,1)S(1)}, u32[]{:S(2)}, u32[]{:S(2)}) %all-to-all-start) | async-done | bytes 196640 | tf_op jit(solution)/shard_map/all_to_all | solution.py:60
  37.0 0.1 reshape.22
  37.1 0.1 copy.14
  37.2 0.1 reshape.23
  37.4 1.0 broadcast_in_dim.6
  38.4 4.2 %all-to-all-start.1 = ((bf16[4,768,128]{2,1,0:T(8,128)(2,1)}), bf16[4,768,128]{2,1,0:T(8,128)(2,1)S(1)}, u32[]{:S(2)}, u32[]{:S(2)}) async-start(bf16[4,768,128]{2,1,0:T(8,128)(2,1)} %broadcast_in_dim.6), calls=%async_computation.1 | async-start | bytes 1572864 | tf_op jit(solution)/shard_map/all_to_all | solution.py:60
  42.6 3.7 %collective-permute-start.4 = (bf16[64,8192]{1,0:T(8,128)(2,1)}, bf16[64,8192]{1,0:T(8,128)(2,1)}, u32[]{:S(2)}, u32[]{:S(2)}) collective-permute-start(bf16[64,8192]{1,0:T(8,128)(2,1)} %get-tuple-element.11.refs_1_), channel_id=1, source_target_pairs={{0,1},{1,0},{2,3},{3,2},{4,5},{5,4},{6,7},{7,6},{8,9},{9,8},{10,11... | collective-permute-start | bytes 3145736 | tf_op jit(solution)/shard_map/ppermute | solution.py:298
  46.2 1.9 %collective-permute-start.5 = (bf16[64,8192]{1,0:T(8,128)(2,1)}, bf16[64,8192]{1,0:T(8,128)(2,1)}, u32[]{:S(2)}, u32[]{:S(2)}) collective-permute-start(bf16[64,8192]{1,0:T(8,128)(2,1)} %get-tuple-element.12.refs_2_), channel_id=1, source_target_pairs={{0,1},{1,0},{2,3},{3,2},{4,5},{5,4},{6,7},{7,6},{8,9},{9,8},{10,11... | collective-permute-start | bytes 3145736 | tf_op jit(solution)/shard_map/ppermute | solution.py:298
  48.2 3.0 %all-to-all-done.1.refs_8_.refs_0_ = bf16[4,768,128]{2,1,0:T(8,128)(2,1)S(1)} async-done(((bf16[4,768,128]{2,1,0:T(8,128)(2,1)}), bf16[4,768,128]{2,1,0:T(8,128)(2,1)S(1)}, u32[]{:S(2)}, u32[]{:S(2)}) %all-to-all-start.1) | async-done | bytes 786464 | tf_op jit(solution)/shard_map/all_to_all | solution.py:60
  51.2 4.3 %collective-permute-start = (bf16[4,768,128]{2,1,0:T(8,128)(2,1)S(1)}, bf16[4,768,128]{2,1,0:T(8,128)(2,1)}, u32[]{:S(2)}, u32[]{:S(2)}) collective-permute-start(bf16[4,768,128]{2,1,0:T(8,128)(2,1)S(1)} %all-to-all-done.1.refs_8_.refs_0_), channel_id=1, source_target_pairs={{0,8},{1,3},{2,10},{3,1},{4,12},{5,7},{6,14},{7,5},{8,0},{9,11},{1... | collective-permute-start | bytes 2359304 | tf_op jit(solution)/shard_map/ppermute | solution.py:300
  55.6 2.2 %collective-permute-start.1 = (bf16[4,768,128]{2,1,0:T(8,128)(2,1)S(1)}, bf16[4,768,128]{2,1,0:T(8,128)(2,1)}, u32[]{:S(2)}, u32[]{:S(2)}) collective-permute-start(bf16[4,768,128]{2,1,0:T(8,128)(2,1)S(1)} %all-to-all-done.1.refs_8_.refs_0_), channel_id=1, source_target_pairs={{0,4},{1,17},{2,6},{3,19},{4,8},{5,21},{6,10},{7,23},{8,12},{9,25}... | collective-permute-start | bytes 2359304 | tf_op jit(solution)/shard_map/ppermute | solution.py:300
  57.8 0.0 collective-permute-done.3.refs_3_
  57.8 4.3 %collective-permute-start.2 = (bf16[4,768,128]{2,1,0:T(8,128)(2,1)S(1)}, bf16[4,768,128]{2,1,0:T(8,128)(2,1)}, u32[]{:S(2)}, u32[]{:S(2)}) collective-permute-start(bf16[4,768,128]{2,1,0:T(8,128)(2,1)S(1)} %all-to-all-done.1.refs_8_.refs_0_), channel_id=1, source_target_pairs={{0,12},{1,19},{2,14},{3,17},{4,0},{5,23},{6,2},{7,21},{8,4},{9,27}... | collective-permute-start | bytes 2359304 | tf_op jit(solution)/shard_map/ppermute | solution.py:300
  62.5 0.1 stack.67.dest_ref
  62.6 0.0 collective-permute-done.4.refs_4_
  62.6 0.0 collective-permute-done.5.refs_5_
  62.6 0.0 copy-done
  62.6 0.0 copy-done.1
  62.6 0.0 copy-start.2
  62.6 1.2 copy-done.2
  63.9 0.0 copy-start.3
  63.9 1.2 copy-done.3
  65.1 0.0 copy-start.4
  65.1 1.2 copy-done.4
  66.3 2.1 %shard_map.111.refs_4_ = bf16[512,8192]{1,0:T(8,128)(2,1)S(1)} custom-call(bf16[64,8192]{1,0:T(8,128)(2,1)S(1)} %copy-done.2, bf16[64,8192]{1,0:T(8,128)(2,1)S(1)} %copy-done.3, bf16[64,8192]{1,0:T(8,128)(2,1)S(1)} %copy-done.4, bf16[64,8192]{1,0:T(8,128)(2,1)} %collective-permute-done.3.refs_3_, bf16[64,8192]{1,0:T(8,128)(2,1)} %collective-permute-done.4.refs_4_, ...), custom_call_target="tpu_custom_call" | custom-call | bytes 16777216 | tf_op jit(solution)/shard_map/pallas_call | solution.py:179
  68.4 0.0 copy-start.5
  68.5 0.0 collective-permute-done.refs_1_
  68.5 5.8 %collective-permute-done.1.refs_2_ = bf16[4,768,128]{2,1,0:T(8,128)(2,1)} collective-permute-done((bf16[4,768,128]{2,1,0:T(8,128)(2,1)S(1)}, bf16[4,768,128]{2,1,0:T(8,128)(2,1)}, u32[]{:S(2)}, u32[]{:S(2)}) %collective-permute-start.1) | collective-permute-done | bytes 786464 | tf_op jit(solution)/shard_map/ppermute | solution.py:300
  74.3 0.0 collective-permute-done.2.refs_3_
  74.3 4.8 %shard_map.112 = (f32[16,3,4,128]{3,2,1,0:T(4,128)S(1)}, f32[128,128]{1,0:T(8,128)S(1)}) custom-call(s32[16]{0:T(128)S(1)} %stack.67.dest_ref, bf16[4,768,128]{2,1,0:T(8,128)(2,1)S(1)} %all-to-all-done.1.refs_8_.refs_0_, bf16[4,768,128]{2,1,0:T(8,128)(2,1)} %collective-permute-done.refs_1_, bf16[4,768,128]{2,1,0:T(8,128)(2,1)} %collective-permute-done.1.refs_2_, ...), custom_call_target="tpu_custom_call" | custom-call | flops 2147483648 | bytes 12582912 | tf_op jit(solution)/shard_map/pallas_call | solution.py:147
  79.1 11.1 %all_to_all.25 = f32[16,3,4,128]{3,2,1,0:T(4,128)S(1)} all-to-all(f32[16,3,4,128]{3,2,1,0:T(4,128)S(1)} %get-tuple-element.13), channel_id=1, replica_groups={{0,2,4,6,8,10,12,14,16,18,20,22,24,26,28,30},{1,3,5,7,9,11,13,15,17,19,..., dimensions={0} | all-to-all | bytes 196608 | tf_op jit(solution)/shard_map/all_to_all | solution.py:60
  90.2 14.4 %all_to_all.26 = f32[16,3,4,128]{3,2,1,0:T(4,128)S(1)} all-to-all(f32[16,3,4,128]{3,2,1,0:T(4,128)S(1)} %broadcast_in_dim.7), channel_id=1, replica_groups={{0,32,64,96,128,160,192,224,256,288,320,352,384,416,448,480},{1,33,65,9..., dimensions={0} | all-to-all | bytes 196608 | tf_op jit(solution)/shard_map/all_to_all | solution.py:60
  104.7 0.7 broadcast_in_dim.8
  105.4 10.0 %all-to-all-start.4 = ((f32[32,3,4,128]{3,2,1,0:T(4,128)}), f32[32,3,4,128]{3,2,1,0:T(4,128)S(1)}, u32[]{:S(2)}, u32[]{:S(2)}) async-start(f32[32,3,4,128]{3,2,1,0:T(4,128)} %broadcast_in_dim.8), calls=%async_computation.4 | async-start | bytes 393216 | tf_op jit(solution)/shard_map/all_to_all | solution.py:60
  115.4 0.0 copy-done.5
  115.4 0.1 reshape.25
  115.5 0.1 pad.4
  115.5 1.9 %all-gather = f32[256,128]{1,0:T(8,128)S(1)} all-gather(f32[128,128]{1,0:T(8,128)S(1)} %get-tuple-element.14), channel_id=2, replica_groups={{0,1},{2,3},{4,5},{6,7},{8,9},{10,11},{12,13},{14,15},{16,17},{18,19},{..., dimensions={0}, use_global_device_ids=true | all-gather | bytes 196608 | tf_op jit(solution)/shard_map/all_gather | solution.py:312
  117.4 6.1 %all-to-all-done.4 = f32[32,3,4,128]{3,2,1,0:T(4,128)S(1)} async-done(((f32[32,3,4,128]{3,2,1,0:T(4,128)}), f32[32,3,4,128]{3,2,1,0:T(4,128)S(1)}, u32[]{:S(2)}, u32[]{:S(2)}) %all-to-all-start.4) | async-done | bytes 196640 | tf_op jit(solution)/shard_map/all_to_all | solution.py:60
  123.6 2.3 %shard_map.113 = f32[3,8,4096]{2,1,0:T(8,128)} custom-call(f32[16,2,3,4,128]{4,3,2,1,0:T(4,128)S(1)} %bitcast.23, f32[2,128,128]{2,1,0:T(8,128)S(1)} %bitcast.24, s32[1,256]{1,0:T(1,128)S(1)} %bitcast.25), custom_call_target="tpu_custom_call" | custom-call | flops 301989888 | bytes 2097152 | tf_op jit(solution)/shard_map/pallas_call | solution.py:266
  (6 shorter events, 0.1 us)
Async XLA Ops:
  0.0 62.6 %copy-start = (bf16[64,8192]{1,0:T(8,128)(2,1)S(1)}, bf16[64,8192]{1,0:T(8,128)(2,1)}, u32[]{:S(2)}) copy-start(bf16[64,8192]{1,0:T(8,128)(2,1)} %refs_6_.1) | copy-start | bytes 3145732
  0.0 62.6 %copy-start.1 = (bf16[64,8192]{1,0:T(8,128)(2,1)S(1)}, bf16[64,8192]{1,0:T(8,128)(2,1)}, u32[]{:S(2)}) copy-start(bf16[64,8192]{1,0:T(8,128)(2,1)} %refs_7_.1) | copy-start | bytes 3145732
  1.6 35.4 %all-to-all-start = ((bf16[32,24,128]{2,1,0:T(8,128)(2,1)}), bf16[32,24,128]{2,1,0:T(8,128)(2,1)S(1)}, u32[]{:S(2)}, u32[]{:S(2)}) async-start(bf16[32,24,128]{2,1,0:T(8,128)(2,1)} %shard_map.109), calls=%async_computation | async-start | bytes 393216 | tf_op jit(solution)/shard_map/all_to_all | solution.py:60
  22.6 35.2 %collective-permute-start.3 = (bf16[64,8192]{1,0:T(8,128)(2,1)}, bf16[64,8192]{1,0:T(8,128)(2,1)}, u32[]{:S(2)}, u32[]{:S(2)}) collective-permute-start(bf16[64,8192]{1,0:T(8,128)(2,1)} %get-tuple-element.10.refs_0_), channel_id=1, source_target_pairs={{0,1},{1,0},{2,3},{3,2},{4,5},{5,4},{6,7},{7,6},{8,9},{9,8},{10,11... | collective-permute-start | bytes 3145736 | tf_op jit(solution)/shard_map/ppermute | solution.py:298
  38.4 12.8 %all-to-all-start.1 = ((bf16[4,768,128]{2,1,0:T(8,128)(2,1)}), bf16[4,768,128]{2,1,0:T(8,128)(2,1)S(1)}, u32[]{:S(2)}, u32[]{:S(2)}) async-start(bf16[4,768,128]{2,1,0:T(8,128)(2,1)} %broadcast_in_dim.6), calls=%async_computation.1 | async-start | bytes 1572864 | tf_op jit(solution)/shard_map/all_to_all | solution.py:60
  42.6 20.0 %collective-permute-start.4 = (bf16[64,8192]{1,0:T(8,128)(2,1)}, bf16[64,8192]{1,0:T(8,128)(2,1)}, u32[]{:S(2)}, u32[]{:S(2)}) collective-permute-start(bf16[64,8192]{1,0:T(8,128)(2,1)} %get-tuple-element.11.refs_1_), channel_id=1, source_target_pairs={{0,1},{1,0},{2,3},{3,2},{4,5},{5,4},{6,7},{7,6},{8,9},{9,8},{10,11... | collective-permute-start | bytes 3145736 | tf_op jit(solution)/shard_map/ppermute | solution.py:298
  46.2 16.4 %collective-permute-start.5 = (bf16[64,8192]{1,0:T(8,128)(2,1)}, bf16[64,8192]{1,0:T(8,128)(2,1)}, u32[]{:S(2)}, u32[]{:S(2)}) collective-permute-start(bf16[64,8192]{1,0:T(8,128)(2,1)} %get-tuple-element.12.refs_2_), channel_id=1, source_target_pairs={{0,1},{1,0},{2,3},{3,2},{4,5},{5,4},{6,7},{7,6},{8,9},{9,8},{10,11... | collective-permute-start | bytes 3145736 | tf_op jit(solution)/shard_map/ppermute | solution.py:298
  51.2 17.2 %collective-permute-start = (bf16[4,768,128]{2,1,0:T(8,128)(2,1)S(1)}, bf16[4,768,128]{2,1,0:T(8,128)(2,1)}, u32[]{:S(2)}, u32[]{:S(2)}) collective-permute-start(bf16[4,768,128]{2,1,0:T(8,128)(2,1)S(1)} %all-to-all-done.1.refs_8_.refs_0_), channel_id=1, source_target_pairs={{0,8},{1,3},{2,10},{3,1},{4,12},{5,7},{6,14},{7,5},{8,0},{9,11},{1... | collective-permute-start | bytes 2359304 | tf_op jit(solution)/shard_map/ppermute | solution.py:300
  55.6 18.7 %collective-permute-start.1 = (bf16[4,768,128]{2,1,0:T(8,128)(2,1)S(1)}, bf16[4,768,128]{2,1,0:T(8,128)(2,1)}, u32[]{:S(2)}, u32[]{:S(2)}) collective-permute-start(bf16[4,768,128]{2,1,0:T(8,128)(2,1)S(1)} %all-to-all-done.1.refs_8_.refs_0_), channel_id=1, source_target_pairs={{0,4},{1,17},{2,6},{3,19},{4,8},{5,21},{6,10},{7,23},{8,12},{9,25}... | collective-permute-start | bytes 2359304 | tf_op jit(solution)/shard_map/ppermute | solution.py:300
  57.8 16.5 %collective-permute-start.2 = (bf16[4,768,128]{2,1,0:T(8,128)(2,1)S(1)}, bf16[4,768,128]{2,1,0:T(8,128)(2,1)}, u32[]{:S(2)}, u32[]{:S(2)}) collective-permute-start(bf16[4,768,128]{2,1,0:T(8,128)(2,1)S(1)} %all-to-all-done.1.refs_8_.refs_0_), channel_id=1, source_target_pairs={{0,12},{1,19},{2,14},{3,17},{4,0},{5,23},{6,2},{7,21},{8,4},{9,27}... | collective-permute-start | bytes 2359304 | tf_op jit(solution)/shard_map/ppermute | solution.py:300
  62.6 1.2 copy-start.2
  63.9 1.2 copy-start.3
  65.1 1.2 copy-start.4
  68.4 46.9 %copy-start.5 = (s32[192]{0:T(256)S(1)}, s32[192]{0:T(256)}, u32[]{:S(2)}) copy-start(s32[192]{0:T(256)} %param.21) | copy-start | bytes 2308
  105.4 18.2 %all-to-all-start.4 = ((f32[32,3,4,128]{3,2,1,0:T(4,128)}), f32[32,3,4,128]{3,2,1,0:T(4,128)S(1)}, u32[]{:S(2)}, u32[]{:S(2)}) async-start(f32[32,3,4,128]{3,2,1,0:T(4,128)} %broadcast_in_dim.8), calls=%async_computation.4 | async-start | bytes 393216 | tf_op jit(solution)/shard_map/all_to_all | solution.py:60

commit v4 on v3

--- a/solution.py
+++ b/solution.py
@@ -36,8 +36,9 @@
 
 
 SITES = [(xl, y, xh) for xl in range(NXL) for y in range(NY) for xh in range(NXH)]
-COLUMN_GROUPS = [[device(z, *s, c) for z in range(NZ) for c in range(NC)] for s in SITES]
-Z_GROUPS = [[device(z, *s, c) for z in range(NZ)] for s in SITES for c in range(NC)]
+ORDER = [(z + NZ // 2) % NZ for z in range(NZ)]
+COLUMN_GROUPS = [[device(z, *s, c) for z in ORDER for c in range(NC)] for s in SITES]
+Z_GROUPS = [[device(z, *s, c) for z in ORDER] for s in SITES for c in range(NC)]
 FIRST_GROUPS = x_groups(0) + y_groups(1)
 SECOND_GROUPS = y_groups(0) + x_groups(1)
 PLANE_GROUPS = [[device(z, *s, c) for s in SITES] for z in range(NZ) for c in range(NC)]
@@ -77,7 +78,8 @@
 
 
 def block_kernel(dest_ref, *refs):
-    lines, w_ref, f_ref, h_ref, x_ref, acc_ref, s_ref = refs[0:4], *refs[4:]
+    lines = refs[0:4]
+    w_ref, f_ref, h_ref, x_ref, acc_ref, s_ref = refs[4:]
     lane16 = lax.broadcasted_iota(jnp.int32, (16, 128), 1)
     first = (lane16 < 64).astype(jnp.float32).astype(jnp.bfloat16)
     second = (lane16 >= 64).astype(jnp.float32).astype(jnp.bfloat16)
@@ -85,8 +87,9 @@
         for k in range(4):
             for j in range(4):
                 place = dest_ref[k * 4 + j]
-                for slab in range(group * SLABS, group * SLABS + SLABS):
-                    base = pl.multiple_of(slab * 512 + place, 32)
+                for z in range(group * SLABS, group * SLABS + SLABS):
+                    slab = ORDER.index(z)
+                    base = pl.multiple_of(z * 512 + place, 32)
                     x_ref[pl.ds(base, 32), 0:128] = lines[k][j, slab * 32 : slab * 32 + 32, :]
                     tile = lines[k][j, 512 + slab * 16 : 528 + slab * 16, :]
                     x_ref[pl.ds(base, 16), 128:256] = tile * first
@@ -184,7 +187,7 @@
         scratch_shapes=[pltpu.SemaphoreType.DMA((8,))],
         compiler_params=pltpu.CompilerParams(vmem_limit_bytes=16 * MIB),
         cost_estimate=pl.CostEstimate(flops=0, bytes_accessed=16 * MIB, transcendentals=0),
-    )(*parts, after)
+    )(*[pltpu.with_memory_space_constraint(part, pltpu.HBM) for part in parts], after)
 
 
 def stack_kernel(*refs):
@@ -248,13 +251,22 @@
         (s_ref[64:128, :], known[0:64]),
         (known[64:128], s_ref[128:192, :]),
     )
+    def parts(side):
+        high = side.astype(jnp.bfloat16).astype(jnp.float32)
+        return high, side - high
+
     for k, (left, right) in enumerate(sides):
-        stacked = jnp.where(inside, left[:, None, :], 0.0).reshape(64 * DOCS, NC * 128)
+        left_high, left_low = [
+            jnp.where(inside, part[:, None, :], 0.0)
+            .reshape(64 * DOCS, NC * 128)
+            .astype(jnp.bfloat16)
+            for part in parts(left)
+        ]
+        right_high, right_low = [part.astype(jnp.bfloat16) for part in parts(right)]
         blocks = lax.dot_general(
-            stacked,
-            right,
+            jnp.concatenate([left_high, left_high, left_low], axis=1),
+            jnp.concatenate([right_high, right_low, right_high], axis=1),
             (((1,), (1,)), ((), ())),
-            precision=lax.Precision.HIGHEST,
             preferred_element_type=jnp.float32,
         )
         for i in range(0, 64, 2):
@@ -269,7 +281,7 @@
         scratch_shapes=[pltpu.VMEM((192, 256), jnp.float32)],
         compiler_params=pltpu.CompilerParams(vmem_limit_bytes=16 * MIB),
         cost_estimate=pl.CostEstimate(
-            flops=2 * 3 * 512 * 256 * 64 * 6, bytes_accessed=2 * MIB, transcendentals=0
+            flops=2 * 3 * 512 * 256 * 64 * 3, bytes_accessed=2 * MIB, transcendentals=0
         ),
     )(factors, known, ids)
 
@@ -297,6 +309,7 @@
     own = stack((gate_weight, up_weight, down_weight), (gate_proj, up_proj, hidden_proj))
     other = [lax.ppermute(part, BOTH, SWAP) for part in own]
     line = spread(column, FIRST_GROUPS)
+    line, *other = lax.optimization_barrier((line, *other))
     lines = [line] + [lax.ppermute(line, BOTH, ring(shift)) for shift in SHIFTS[1:]]
     dest = []
     for shift in SHIFTS:

time: 127 us -> 120 us (0.945)
  waiting for transfers between devices: 27.2 us -> 21.4 us
  local copies, waits for them, and re-layouts: 6 us -> 3.27 us
  starting transfers between devices: 49.4 us -> 50.9 us
    all_to_all x3, waiting for transfers between devices: 21.4 us -> 13.5 us  [exchange(): return lax.all_to_all(blocks, BOTH, 0, 0, axis_index_groups=groups)]
    unnamed x12 -> x6, local copies, waits for them, and re-layouts: 3.68 us -> 0.95 us
    all_to_all x3, starting transfers between devices: 30.9 us -> 33.2 us  [exchange(): return lax.all_to_all(blocks, BOTH, 0, 0, axis_index_groups=groups)]
    ppermute x3, waiting for transfers between devices: 5.81 us -> 7.93 us  [local(): lax.ppermute(line, BOTH, ring(shift))]
    pallas_call x1, Pallas kernels: 2.14 us -> 3.48 us  [load(): pl.pallas_call(load_kernel, in_specs=[pl.BlockSpec(memory_space=pl.ANY)]...]
  transfers between devices with their start and end apart: 9 -> 9, of which waited for: 4 -> 4; matrix products, arithmetic and copies ran while one was open for 1% -> 1% of each run, Pallas kernels for 5% -> 6%
where the time goes in v4:
time: 120 us; the launch traced here: 119 us
  starting transfers between devices  50.9 us (42%)
  blocking collectives  28.2 us (24%)
  waiting for transfers between devices  21.4 us (18%)
  Pallas kernels  14.4 us (12%)
  local copies, waits for them, and re-layouts  3.27 us (3%)
    all_to_all x3, starting transfers between devices, exchange(): return lax.all_to_all(blocks, BOTH, 0, 0, axis_index_groups=groups)  33.2 us
    all_to_all x2, blocking collectives, exchange(): return lax.all_to_all(blocks, BOTH, 0, 0, axis_index_groups=groups)  26.3 us
    all_to_all x3, waiting for transfers between devices, exchange(): return lax.all_to_all(blocks, BOTH, 0, 0, axis_index_groups=groups)  13.5 us
    ppermute x3, starting transfers between devices, local(): lax.ppermute(line, BOTH, ring(shift))  11.1 us
    ppermute x3, waiting for transfers between devices, local(): lax.ppermute(line, BOTH, ring(shift))  7.93 us
    ppermute x3, starting transfers between devices, local(): other = [lax.ppermute(part, BOTH, SWAP) for part in own]  6.58 us
    pallas_call x1, Pallas kernels, stack(): pl.pallas_call(stack_kernel, grid=(8192 // width,), in_specs=[weight] * 3...  4.19 us
    pallas_call x1, Pallas kernels, block(): pl.pallas_call(block_kernel, in_specs=[pl.BlockSpec(memory_space=pltpu.SM...  3.71 us
  transfers between devices with their start and end apart: 9, of which 4 were waited for; matrix products, arithmetic and copies ran while one was open for 1% of the time, Pallas kernels for 6%

profile of v4, /device:TPU:1, one launch (start us, length us, event | category | flops | bytes accessed | tf_op | source)
XLA Modules:
  0.0 118.9 jit_solution(15069902999828119405)
XLA Ops:
  0.0 1.5 %shard_map.109 = bf16[32,24,128]{2,1,0:T(8,128)(2,1)} custom-call(bf16[16,192]{1,0:T(8,128)(2,1)} %bitcast.28, bf16[16,192]{1,0:T(8,128)(2,1)} %bitcast.29), custom_call_target="tpu_custom_call" | custom-call | bytes 262144 | tf_op jit(solution)/shard_map/pallas_call | solution.py:233
  1.5 20.1 %all-to-all-start = ((bf16[32,24,128]{2,1,0:T(8,128)(2,1)}), bf16[32,24,128]{2,1,0:T(8,128)(2,1)S(1)}, u32[]{:S(2)}, u32[]{:S(2)}) async-start(bf16[32,24,128]{2,1,0:T(8,128)(2,1)} %shard_map.109), calls=%async_computation | async-start | bytes 393216 | tf_op jit(solution)/shard_map/all_to_all | solution.py:61
  21.6 4.2 %shard_map.110 = (bf16[64,8192]{1,0:T(8,128)(2,1)}, bf16[64,8192]{1,0:T(8,128)(2,1)}, bf16[64,8192]{1,0:T(8,128)(2,1)}) custom-call(bf16[56,8192]{1,0:T(8,128)(2,1)} %refs_0_.1, bf16[56,8192]{1,0:T(8,128)(2,1)} %refs_1_.1, bf16[56,8192]{1,0:T(8,128)(2,1)} %refs_2_.1, bf16[56,64]{1,0:T(8,128)(2,1)} %refs_3_.1, bf16[56,64]{1,0:T(8,128)(2,1)} %refs_4_.1, ...), custom_call_target="tpu_custom_call" | custom-call | bytes 6291456 | tf_op jit(solution)/shard_map/pallas_call | solution.py:210
  25.8 2.3 %collective-permute-start = (bf16[64,8192]{1,0:T(8,128)(2,1)}, bf16[64,8192]{1,0:T(8,128)(2,1)S(1)}, u32[]{:S(2)}, u32[]{:S(2)}) collective-permute-start(bf16[64,8192]{1,0:T(8,128)(2,1)} %get-tuple-element.14.refs_0_), channel_id=1, source_target_pairs={{0,1},{1,0},{2,3},{3,2},{4,5},{5,4},{6,7},{7,6},{8,9},{9,8},{10,11... | collective-permute-start | bytes 3145736 | tf_op jit(solution)/shard_map/ppermute | solution.py:310
  28.1 2.1 %collective-permute-start.1 = (bf16[64,8192]{1,0:T(8,128)(2,1)}, bf16[64,8192]{1,0:T(8,128)(2,1)S(1)}, u32[]{:S(2)}, u32[]{:S(2)}) collective-permute-start(bf16[64,8192]{1,0:T(8,128)(2,1)} %get-tuple-element.15.refs_1_), channel_id=1, source_target_pairs={{0,1},{1,0},{2,3},{3,2},{4,5},{5,4},{6,7},{7,6},{8,9},{9,8},{10,11... | collective-permute-start | bytes 3145736 | tf_op jit(solution)/shard_map/ppermute | solution.py:310
  30.1 2.3 %collective-permute-start.2 = (bf16[64,8192]{1,0:T(8,128)(2,1)}, bf16[64,8192]{1,0:T(8,128)(2,1)}, u32[]{:S(2)}, u32[]{:S(2)}) collective-permute-start(bf16[64,8192]{1,0:T(8,128)(2,1)} %get-tuple-element.16.refs_2_), channel_id=1, source_target_pairs={{0,1},{1,0},{2,3},{3,2},{4,5},{5,4},{6,7},{7,6},{8,9},{9,8},{10,11... | collective-permute-start | bytes 3145736 | tf_op jit(solution)/shard_map/ppermute | solution.py:310
  32.4 0.0 all-to-all-done
  32.5 0.1 reshape.22
  32.6 0.1 copy.14
  32.7 0.1 reshape.23
  32.8 1.0 broadcast_in_dim.6
  33.8 4.2 %all-to-all-start.1 = ((bf16[4,768,128]{2,1,0:T(8,128)(2,1)}), bf16[4,768,128]{2,1,0:T(8,128)(2,1)S(1)}, u32[]{:S(2)}, u32[]{:S(2)}) async-start(bf16[4,768,128]{2,1,0:T(8,128)(2,1)} %broadcast_in_dim.6), calls=%async_computation.1 | async-start | bytes 1572864 | tf_op jit(solution)/shard_map/all_to_all | solution.py:61
  38.0 0.0 collective-permute-done.refs_3_
  38.0 0.0 copy-start
  38.0 0.0 collective-permute-done.1.refs_4_
  38.0 0.0 copy-start.1
  38.0 0.0 collective-permute-done.2.refs_5_
  38.1 0.9 copy-done
  39.0 7.4 %all-to-all-done.1.refs_8_.refs_0_ = bf16[4,768,128]{2,1,0:T(8,128)(2,1)S(1)} async-done(((bf16[4,768,128]{2,1,0:T(8,128)(2,1)}), bf16[4,768,128]{2,1,0:T(8,128)(2,1)S(1)}, u32[]{:S(2)}, u32[]{:S(2)}) %all-to-all-start.1) | async-done | bytes 786464 | tf_op jit(solution)/shard_map/all_to_all | solution.py:61
  46.4 0.0 copy-done.1
  46.4 4.6 %collective-permute-start.3 = (bf16[4,768,128]{2,1,0:T(8,128)(2,1)S(1)}, bf16[4,768,128]{2,1,0:T(8,128)(2,1)S(1)}, u32[]{:S(2)}, u32[]{:S(2)}) collective-permute-start(bf16[4,768,128]{2,1,0:T(8,128)(2,1)S(1)} %all-to-all-done.1.refs_8_.refs_0_), channel_id=1, source_target_pairs={{0,8},{1,3},{2,10},{3,1},{4,12},{5,7},{6,14},{7,5},{8,0},{9,11},{1... | collective-permute-start | bytes 2359304 | tf_op jit(solution)/shard_map/ppermute | solution.py:313
  51.0 2.2 %collective-permute-start.4 = (bf16[4,768,128]{2,1,0:T(8,128)(2,1)S(1)}, bf16[4,768,128]{2,1,0:T(8,128)(2,1)S(1)}, u32[]{:S(2)}, u32[]{:S(2)}) collective-permute-start(bf16[4,768,128]{2,1,0:T(8,128)(2,1)S(1)} %all-to-all-done.1.refs_8_.refs_0_), channel_id=1, source_target_pairs={{0,4},{1,17},{2,6},{3,19},{4,8},{5,21},{6,10},{7,23},{8,12},{9,25}... | collective-permute-start | bytes 2359304 | tf_op jit(solution)/shard_map/ppermute | solution.py:313
  53.2 4.3 %collective-permute-start.5 = (bf16[4,768,128]{2,1,0:T(8,128)(2,1)S(1)}, bf16[4,768,128]{2,1,0:T(8,128)(2,1)S(1)}, u32[]{:S(2)}, u32[]{:S(2)}) collective-permute-start(bf16[4,768,128]{2,1,0:T(8,128)(2,1)S(1)} %all-to-all-done.1.refs_8_.refs_0_), channel_id=1, source_target_pairs={{0,12},{1,19},{2,14},{3,17},{4,0},{5,23},{6,2},{7,21},{8,4},{9,27}... | collective-permute-start | bytes 2359304 | tf_op jit(solution)/shard_map/ppermute | solution.py:313
  57.9 0.1 stack.67.dest_ref
  58.0 3.5 %shard_map.111.refs_4_ = bf16[512,8192]{1,0:T(8,128)(2,1)S(1)} custom-call(bf16[64,8192]{1,0:T(8,128)(2,1)} %get-tuple-element.14.refs_0_, bf16[64,8192]{1,0:T(8,128)(2,1)} %get-tuple-element.15.refs_1_, bf16[64,8192]{1,0:T(8,128)(2,1)} %get-tuple-element.16.refs_2_, bf16[64,8192]{1,0:T(8,128)(2,1)} %copy-done, bf16[64,8192]{1,0:T(8,128)(2,1)} %copy-done.1, ...), custom_call_target="tpu_custom_call" | custom-call | bytes 16777216 | tf_op jit(solution)/shard_map/pallas_call | solution.py:182
  61.5 0.0 copy-start.2
  61.5 0.0 collective-permute-done.3.refs_1_
  61.5 7.8 %collective-permute-done.4.refs_2_ = bf16[4,768,128]{2,1,0:T(8,128)(2,1)S(1)} collective-permute-done((bf16[4,768,128]{2,1,0:T(8,128)(2,1)S(1)}, bf16[4,768,128]{2,1,0:T(8,128)(2,1)S(1)}, u32[]{:S(2)}, u32[]{:S(2)}) %collective-permute-start.4) | collective-permute-done | bytes 786464 | tf_op jit(solution)/shard_map/ppermute | solution.py:313
  69.3 0.1 collective-permute-done.5.refs_3_
  69.4 3.7 %shard_map.112 = (f32[16,3,4,128]{3,2,1,0:T(4,128)S(1)}, f32[128,128]{1,0:T(8,128)S(1)}) custom-call(s32[16]{0:T(128)S(1)} %stack.67.dest_ref, bf16[4,768,128]{2,1,0:T(8,128)(2,1)S(1)} %all-to-all-done.1.refs_8_.refs_0_, bf16[4,768,128]{2,1,0:T(8,128)(2,1)S(1)} %collective-permute-done.3.refs_1_, bf16[4,768,128]{2,1,0:T(8,128)(2,1)S(1)} %collective-permute-done.4.refs_2_, ...), custom_call_target="tpu_custom_call" | custom-call | flops 2147483648 | bytes 12582912 | tf_op jit(solution)/shard_map/pallas_call | solution.py:150
  73.2 11.2 %all_to_all.25 = f32[16,3,4,128]{3,2,1,0:T(4,128)S(1)} all-to-all(f32[16,3,4,128]{3,2,1,0:T(4,128)S(1)} %get-tuple-element.21), channel_id=1, replica_groups={{0,2,4,6,8,10,12,14,16,18,20,22,24,26,28,30},{1,3,5,7,9,11,13,15,17,19,..., dimensions={0} | all-to-all | bytes 196608 | tf_op jit(solution)/shard_map/all_to_all | solution.py:61
  84.4 15.1 %all_to_all.26 = f32[16,3,4,128]{3,2,1,0:T(4,128)S(1)} all-to-all(f32[16,3,4,128]{3,2,1,0:T(4,128)S(1)} %broadcast_in_dim.7), channel_id=1, replica_groups={{256,288,320,352,384,416,448,480,0,32,64,96,128,160,192,224},{257,289,3..., dimensions={0} | all-to-all | bytes 196608 | tf_op jit(solution)/shard_map/all_to_all | solution.py:61
  99.6 0.7 broadcast_in_dim.8
  100.3 8.8 %all-to-all-start.4 = ((f32[32,3,4,128]{3,2,1,0:T(4,128)}), f32[32,3,4,128]{3,2,1,0:T(4,128)S(1)}, u32[]{:S(2)}, u32[]{:S(2)}) async-start(f32[32,3,4,128]{3,2,1,0:T(4,128)} %broadcast_in_dim.8), calls=%async_computation.4 | async-start | bytes 393216 | tf_op jit(solution)/shard_map/all_to_all | solution.py:61
  109.1 0.0 copy-done.2
  109.1 0.1 reshape.25
  109.2 0.1 pad.4
  109.3 1.9 %all-gather = f32[256,128]{1,0:T(8,128)S(1)} all-gather(f32[128,128]{1,0:T(8,128)S(1)} %get-tuple-element.22), channel_id=2, replica_groups={{0,1},{2,3},{4,5},{6,7},{8,9},{10,11},{12,13},{14,15},{16,17},{18,19},{..., dimensions={0}, use_global_device_ids=true | all-gather | bytes 196608 | tf_op jit(solution)/shard_map/all_gather | solution.py:325
  111.2 6.1 %all-to-all-done.4 = f32[32,3,4,128]{3,2,1,0:T(4,128)S(1)} async-done(((f32[32,3,4,128]{3,2,1,0:T(4,128)}), f32[32,3,4,128]{3,2,1,0:T(4,128)S(1)}, u32[]{:S(2)}, u32[]{:S(2)}) %all-to-all-start.4) | async-done | bytes 196640 | tf_op jit(solution)/shard_map/all_to_all | solution.py:61
  117.3 1.6 %shard_map.113 = f32[3,8,4096]{2,1,0:T(8,128)} custom-call(f32[16,2,3,4,128]{4,3,2,1,0:T(4,128)S(1)} %bitcast.23, f32[2,128,128]{2,1,0:T(8,128)S(1)} %bitcast.24, s32[1,256]{1,0:T(1,128)S(1)} %bitcast.25), custom_call_target="tpu_custom_call" | custom-call | flops 150994944 | bytes 2097152 | tf_op jit(solution)/shard_map/pallas_call | solution.py:278
  (6 shorter events, 0.1 us)
Async XLA Ops:
  1.5 30.9 %all-to-all-start = ((bf16[32,24,128]{2,1,0:T(8,128)(2,1)}), bf16[32,24,128]{2,1,0:T(8,128)(2,1)S(1)}, u32[]{:S(2)}, u32[]{:S(2)}) async-start(bf16[32,24,128]{2,1,0:T(8,128)(2,1)} %shard_map.109), calls=%async_computation | async-start | bytes 393216 | tf_op jit(solution)/shard_map/all_to_all | solution.py:61
  25.8 12.2 %collective-permute-start = (bf16[64,8192]{1,0:T(8,128)(2,1)}, bf16[64,8192]{1,0:T(8,128)(2,1)S(1)}, u32[]{:S(2)}, u32[]{:S(2)}) collective-permute-start(bf16[64,8192]{1,0:T(8,128)(2,1)} %get-tuple-element.14.refs_0_), channel_id=1, source_target_pairs={{0,1},{1,0},{2,3},{3,2},{4,5},{5,4},{6,7},{7,6},{8,9},{9,8},{10,11... | collective-permute-start | bytes 3145736 | tf_op jit(solution)/shard_map/ppermute | solution.py:310
  28.1 9.9 %collective-permute-start.1 = (bf16[64,8192]{1,0:T(8,128)(2,1)}, bf16[64,8192]{1,0:T(8,128)(2,1)S(1)}, u32[]{:S(2)}, u32[]{:S(2)}) collective-permute-start(bf16[64,8192]{1,0:T(8,128)(2,1)} %get-tuple-element.15.refs_1_), channel_id=1, source_target_pairs={{0,1},{1,0},{2,3},{3,2},{4,5},{5,4},{6,7},{7,6},{8,9},{9,8},{10,11... | collective-permute-start | bytes 3145736 | tf_op jit(solution)/shard_map/ppermute | solution.py:310
  30.1 7.9 %collective-permute-start.2 = (bf16[64,8192]{1,0:T(8,128)(2,1)}, bf16[64,8192]{1,0:T(8,128)(2,1)}, u32[]{:S(2)}, u32[]{:S(2)}) collective-permute-start(bf16[64,8192]{1,0:T(8,128)(2,1)} %get-tuple-element.16.refs_2_), channel_id=1, source_target_pairs={{0,1},{1,0},{2,3},{3,2},{4,5},{5,4},{6,7},{7,6},{8,9},{9,8},{10,11... | collective-permute-start | bytes 3145736 | tf_op jit(solution)/shard_map/ppermute | solution.py:310
  33.8 12.5 %all-to-all-start.1 = ((bf16[4,768,128]{2,1,0:T(8,128)(2,1)}), bf16[4,768,128]{2,1,0:T(8,128)(2,1)S(1)}, u32[]{:S(2)}, u32[]{:S(2)}) async-start(bf16[4,768,128]{2,1,0:T(8,128)(2,1)} %broadcast_in_dim.6), calls=%async_computation.1 | async-start | bytes 1572864 | tf_op jit(solution)/shard_map/all_to_all | solution.py:61
  38.0 1.0 copy-start
  38.0 8.3 %copy-start.1 = (bf16[64,8192]{1,0:T(8,128)(2,1)}, bf16[64,8192]{1,0:T(8,128)(2,1)S(1)}, u32[]{:S(2)}) copy-start(bf16[64,8192]{1,0:T(8,128)(2,1)S(1)} %collective-permute-done.1.refs_4_) | copy-start | bytes 3145732
  46.4 15.1 %collective-permute-start.3 = (bf16[4,768,128]{2,1,0:T(8,128)(2,1)S(1)}, bf16[4,768,128]{2,1,0:T(8,128)(2,1)S(1)}, u32[]{:S(2)}, u32[]{:S(2)}) collective-permute-start(bf16[4,768,128]{2,1,0:T(8,128)(2,1)S(1)} %all-to-all-done.1.refs_8_.refs_0_), channel_id=1, source_target_pairs={{0,8},{1,3},{2,10},{3,1},{4,12},{5,7},{6,14},{7,5},{8,0},{9,11},{1... | collective-permute-start | bytes 2359304 | tf_op jit(solution)/shard_map/ppermute | solution.py:313
  51.0 18.3 %collective-permute-start.4 = (bf16[4,768,128]{2,1,0:T(8,128)(2,1)S(1)}, bf16[4,768,128]{2,1,0:T(8,128)(2,1)S(1)}, u32[]{:S(2)}, u32[]{:S(2)}) collective-permute-start(bf16[4,768,128]{2,1,0:T(8,128)(2,1)S(1)} %all-to-all-done.1.refs_8_.refs_0_), channel_id=1, source_target_pairs={{0,4},{1,17},{2,6},{3,19},{4,8},{5,21},{6,10},{7,23},{8,12},{9,25}... | collective-permute-start | bytes 2359304 | tf_op jit(solution)/shard_map/ppermute | solution.py:313
  53.2 16.2 %collective-permute-start.5 = (bf16[4,768,128]{2,1,0:T(8,128)(2,1)S(1)}, bf16[4,768,128]{2,1,0:T(8,128)(2,1)S(1)}, u32[]{:S(2)}, u32[]{:S(2)}) collective-permute-start(bf16[4,768,128]{2,1,0:T(8,128)(2,1)S(1)} %all-to-all-done.1.refs_8_.refs_0_), channel_id=1, source_target_pairs={{0,12},{1,19},{2,14},{3,17},{4,0},{5,23},{6,2},{7,21},{8,4},{9,27}... | collective-permute-start | bytes 2359304 | tf_op jit(solution)/shard_map/ppermute | solution.py:313
  61.5 47.6 %copy-start.2 = (s32[192]{0:T(256)S(1)}, s32[192]{0:T(256)}, u32[]{:S(2)}) copy-start(s32[192]{0:T(256)} %param.21) | copy-start | bytes 2308
  100.3 17.1 %all-to-all-start.4 = ((f32[32,3,4,128]{3,2,1,0:T(4,128)}), f32[32,3,4,128]{3,2,1,0:T(4,128)S(1)}, u32[]{:S(2)}, u32[]{:S(2)}) async-start(f32[32,3,4,128]{3,2,1,0:T(4,128)} %broadcast_in_dim.8), calls=%async_computation.4 | async-start | bytes 393216 | tf_op jit(solution)/shard_map/all_to_all | solution.py:61

commit v5 on v4

--- a/solution.py
+++ b/solution.py
@@ -42,7 +42,8 @@
 FIRST_GROUPS = x_groups(0) + y_groups(1)
 SECOND_GROUPS = y_groups(0) + x_groups(1)
 PLANE_GROUPS = [[device(z, *s, c) for s in SITES] for z in range(NZ) for c in range(NC)]
-LAYER_GROUPS = [[device(z, *s, c) for s in SITES for c in range(NC)] for z in range(NZ)]
+LAST = [(xl, (y + NY // 2) % NY, 1 - xh) for xl, y, xh in SITES]
+LAYER_GROUPS = [[device(z, *s, c) for s in LAST for c in range(NC)] for z in range(NZ)]
 PAIRS = [[2 * i, 2 * i + 1] for i in range(NZ * PLANE)]
 SWAP = [(i, i ^ 1) for i in range(NZ * PLANE * NC)]
 
@@ -217,6 +218,34 @@
     )(*weights, *projections)
 
 
+def unpack_kernel(column_ref, out_ref):
+    left = lax.broadcasted_iota(jnp.int32, (8, 128), 1) < 64
+    for z in range(NZ):
+        halves = []
+        for c in range(NC):
+            place = z * NC + c
+            wide = column_ref[place, 0:16, :]
+            halves.append(column_ref[place, 16:24, :].astype(jnp.float32))
+            for n in range(4):
+                out_ref[n, place * 16 : place * 16 + 16, :] = wide
+        top = jnp.where(left, halves[0], pltpu.roll(halves[1], 64, 1))
+        low = jnp.where(left, pltpu.roll(halves[0], 64, 1), halves[1])
+        rest = jnp.concatenate([top, low], axis=0).astype(jnp.bfloat16)
+        for n in range(4):
+            out_ref[n, 512 + z * 16 : 528 + z * 16, :] = rest
+
+
+def unpack(column):
+    inside = pl.BlockSpec(memory_space=pltpu.VMEM)
+    return pl.pallas_call(
+        unpack_kernel,
+        in_specs=[inside],
+        out_specs=inside,
+        out_shape=jax.ShapeDtypeStruct((4, 768, 128), jnp.bfloat16),
+        cost_estimate=pl.CostEstimate(flops=0, bytes_accessed=MIB, transcendentals=0),
+    )(pltpu.with_memory_space_constraint(column, pltpu.VMEM))
+
+
 def pack_kernel(t_ref, g_ref, out_ref):
     t, g = t_ref[...].astype(jnp.float32), g_ref[...].astype(jnp.float32)
     for c in range(NC):
@@ -242,7 +271,7 @@
         for c in range(NC):
             for r in range(3):
                 row = p * 12 + r * 4
-                s_ref[row : row + 4, c * 128 : c * 128 + 128] = f_ref[p, c, r]
+                s_ref[row : row + 4, c * 128 : c * 128 + 128] = f_ref[LAST.index(SITES[p]), c, r]
     known = jnp.concatenate([h_ref[0], h_ref[1]], axis=1)
     doc = lax.broadcasted_iota(jnp.int32, (DOCS, NC * 128), 0)
     inside = (ids_ref[...] == doc)[None]
@@ -302,13 +331,9 @@
     me = lax.axis_index("dp") * 16 + lax.axis_index("mp")
     core, x, y = me % NC, me // 2 % NXH * NXL + me // 16 % NXL, me // 4 % NY
     column = exchange(pack(tokens.T, out_grad.T), COLUMN_GROUPS)
-    wide = column[:, :16, :].reshape(512, 128)
-    rest = column[:, 16:, :].reshape(NZ, NC, 8, 2, 64)
-    rest = rest.transpose(0, 3, 2, 1, 4).reshape(256, 128)
-    column = jnp.concatenate([wide, rest], axis=0)
     own = stack((gate_weight, up_weight, down_weight), (gate_proj, up_proj, hidden_proj))
     other = [lax.ppermute(part, BOTH, SWAP) for part in own]
-    line = spread(column, FIRST_GROUPS)
+    line = exchange(unpack(column), FIRST_GROUPS)
     line, *other = lax.optimization_barrier((line, *other))
     lines = [line] + [lax.ppermute(line, BOTH, ring(shift)) for shift in SHIFTS[1:]]
     dest = []

time: 120 us -> 118 us (0.983)
  waiting for transfers between devices: 21.4 us -> 16.9 us
  starting transfers between devices: 50.9 us -> 54.4 us
  local copies, waits for them, and re-layouts: 3.27 us -> 1.93 us
    all_to_all x3, waiting for transfers between devices: 13.5 us -> 8.95 us  [exchange(): return lax.all_to_all(blocks, BOTH, 0, 0, axis_index_groups=groups)]
    all_to_all x3, starting transfers between devices: 33.2 us -> 36.7 us  [exchange(): return lax.all_to_all(blocks, BOTH, 0, 0, axis_index_groups=groups)]
  transfers between devices with their start and end apart: 9 -> 9, of which waited for: 4 -> 4; matrix products, arithmetic and copies ran while one was open for 1% -> 0% of each run, Pallas kernels for 6% -> 7%
where the time goes in v5:
time: 118 us; the launch traced here: 117 us
  starting transfers between devices  54.4 us (46%)
  blocking collectives  28.2 us (24%)
  waiting for transfers between devices  16.9 us (14%)
  Pallas kernels  15.4 us (13%)
  local copies, waits for them, and re-layouts  1.93 us (2%)
    all_to_all x3, starting transfers between devices, exchange(): return lax.all_to_all(blocks, BOTH, 0, 0, axis_index_groups=groups)  36.7 us
    all_to_all x2, blocking collectives, exchange(): return lax.all_to_all(blocks, BOTH, 0, 0, axis_index_groups=groups)  26.3 us
    ppermute x3, starting transfers between devices, local(): lax.ppermute(line, BOTH, ring(shift))  11.1 us
    all_to_all x3, waiting for transfers between devices, exchange(): return lax.all_to_all(blocks, BOTH, 0, 0, axis_index_groups=groups)  8.95 us
    ppermute x3, waiting for transfers between devices, local(): lax.ppermute(line, BOTH, ring(shift))  7.93 us
    ppermute x3, starting transfers between devices, local(): other = [lax.ppermute(part, BOTH, SWAP) for part in own]  6.58 us
    pallas_call x1, Pallas kernels, stack(): pl.pallas_call(stack_kernel, grid=(8192 // width,), in_specs=[weight] * 3...  4.19 us
    pallas_call x1, Pallas kernels, block(): pl.pallas_call(block_kernel, in_specs=[pl.BlockSpec(memory_space=pltpu.SM...  3.71 us
  transfers between devices with their start and end apart: 9, of which 4 were waited for; matrix products, arithmetic and copies ran while one was open for 0% of the time, Pallas kernels for 7%

profile of v5, /device:TPU:1, one launch (start us, length us, event | category | flops | bytes accessed | tf_op | source)
XLA Modules:
  0.0 117.5 jit_solution(5769773614382025390)
XLA Ops:
  0.0 1.5 %shard_map.109 = bf16[32,24,128]{2,1,0:T(8,128)(2,1)} custom-call(bf16[16,192]{1,0:T(8,128)(2,1)} %bitcast.24, bf16[16,192]{1,0:T(8,128)(2,1)} %bitcast.25), custom_call_target="tpu_custom_call" | custom-call | bytes 262144 | tf_op jit(solution)/shard_map/pallas_call | solution.py:262
  1.5 20.1 %all-to-all-start = ((bf16[32,24,128]{2,1,0:T(8,128)(2,1)}), bf16[32,24,128]{2,1,0:T(8,128)(2,1)S(1)}, u32[]{:S(2)}, u32[]{:S(2)}) async-start(bf16[32,24,128]{2,1,0:T(8,128)(2,1)} %shard_map.109), calls=%async_computation | async-start | bytes 393216 | tf_op jit(solution)/shard_map/all_to_all | solution.py:62
  21.6 4.2 %shard_map.111 = (bf16[64,8192]{1,0:T(8,128)(2,1)}, bf16[64,8192]{1,0:T(8,128)(2,1)}, bf16[64,8192]{1,0:T(8,128)(2,1)}) custom-call(bf16[56,8192]{1,0:T(8,128)(2,1)} %refs_0_.1, bf16[56,8192]{1,0:T(8,128)(2,1)} %refs_1_.1, bf16[56,8192]{1,0:T(8,128)(2,1)} %refs_2_.1, bf16[56,64]{1,0:T(8,128)(2,1)} %refs_3_.1, bf16[56,64]{1,0:T(8,128)(2,1)} %refs_4_.1, ...), custom_call_target="tpu_custom_call" | custom-call | bytes 6291456 | tf_op jit(solution)/shard_map/pallas_call | solution.py:211
  25.8 2.3 %collective-permute-start = (bf16[64,8192]{1,0:T(8,128)(2,1)}, bf16[64,8192]{1,0:T(8,128)(2,1)S(1)}, u32[]{:S(2)}, u32[]{:S(2)}) collective-permute-start(bf16[64,8192]{1,0:T(8,128)(2,1)} %get-tuple-element.14.refs_0_), channel_id=1, source_target_pairs={{0,1},{1,0},{2,3},{3,2},{4,5},{5,4},{6,7},{7,6},{8,9},{9,8},{10,11... | collective-permute-start | bytes 3145736 | tf_op jit(solution)/shard_map/ppermute | solution.py:335
  28.1 2.1 %collective-permute-start.1 = (bf16[64,8192]{1,0:T(8,128)(2,1)}, bf16[64,8192]{1,0:T(8,128)(2,1)S(1)}, u32[]{:S(2)}, u32[]{:S(2)}) collective-permute-start(bf16[64,8192]{1,0:T(8,128)(2,1)} %get-tuple-element.15.refs_1_), channel_id=1, source_target_pairs={{0,1},{1,0},{2,3},{3,2},{4,5},{5,4},{6,7},{7,6},{8,9},{9,8},{10,11... | collective-permute-start | bytes 3145736 | tf_op jit(solution)/shard_map/ppermute | solution.py:335
  30.1 2.3 %collective-permute-start.2 = (bf16[64,8192]{1,0:T(8,128)(2,1)}, bf16[64,8192]{1,0:T(8,128)(2,1)}, u32[]{:S(2)}, u32[]{:S(2)}) collective-permute-start(bf16[64,8192]{1,0:T(8,128)(2,1)} %get-tuple-element.16.refs_2_), channel_id=1, source_target_pairs={{0,1},{1,0},{2,3},{3,2},{4,5},{5,4},{6,7},{7,6},{8,9},{9,8},{10,11... | collective-permute-start | bytes 3145736 | tf_op jit(solution)/shard_map/ppermute | solution.py:335
  32.4 0.0 all-to-all-done.column_ref
  32.4 1.0 shard_map.110
  33.4 4.2 %all-to-all-start.1 = ((bf16[4,768,128]{2,1,0:T(8,128)(2,1)}), bf16[4,768,128]{2,1,0:T(8,128)(2,1)S(1)}, u32[]{:S(2)}, u32[]{:S(2)}) async-start(bf16[4,768,128]{2,1,0:T(8,128)(2,1)} %shard_map.110), calls=%async_computation.1 | async-start | bytes 1572864 | tf_op jit(solution)/shard_map/all_to_all | solution.py:62
  37.6 0.0 collective-permute-done.refs_3_
  37.6 0.0 copy-start
  37.6 0.0 collective-permute-done.1.refs_4_
  37.6 0.0 copy-start.1
  37.6 0.0 collective-permute-done.2.refs_5_
  37.7 0.9 copy-done
  38.6 7.4 %all-to-all-done.1.refs_8_.refs_0_ = bf16[4,768,128]{2,1,0:T(8,128)(2,1)S(1)} async-done(((bf16[4,768,128]{2,1,0:T(8,128)(2,1)}), bf16[4,768,128]{2,1,0:T(8,128)(2,1)S(1)}, u32[]{:S(2)}, u32[]{:S(2)}) %all-to-all-start.1) | async-done | bytes 786464 | tf_op jit(solution)/shard_map/all_to_all | solution.py:62
  46.0 0.0 copy-done.1
  46.0 4.6 %collective-permute-start.3 = (bf16[4,768,128]{2,1,0:T(8,128)(2,1)S(1)}, bf16[4,768,128]{2,1,0:T(8,128)(2,1)S(1)}, u32[]{:S(2)}, u32[]{:S(2)}) collective-permute-start(bf16[4,768,128]{2,1,0:T(8,128)(2,1)S(1)} %all-to-all-done.1.refs_8_.refs_0_), channel_id=1, source_target_pairs={{0,8},{1,3},{2,10},{3,1},{4,12},{5,7},{6,14},{7,5},{8,0},{9,11},{1... | collective-permute-start | bytes 2359304 | tf_op jit(solution)/shard_map/ppermute | solution.py:338
  50.6 2.2 %collective-permute-start.4 = (bf16[4,768,128]{2,1,0:T(8,128)(2,1)S(1)}, bf16[4,768,128]{2,1,0:T(8,128)(2,1)S(1)}, u32[]{:S(2)}, u32[]{:S(2)}) collective-permute-start(bf16[4,768,128]{2,1,0:T(8,128)(2,1)S(1)} %all-to-all-done.1.refs_8_.refs_0_), channel_id=1, source_target_pairs={{0,4},{1,17},{2,6},{3,19},{4,8},{5,21},{6,10},{7,23},{8,12},{9,25}... | collective-permute-start | bytes 2359304 | tf_op jit(solution)/shard_map/ppermute | solution.py:338
  52.8 4.3 %collective-permute-start.5 = (bf16[4,768,128]{2,1,0:T(8,128)(2,1)S(1)}, bf16[4,768,128]{2,1,0:T(8,128)(2,1)S(1)}, u32[]{:S(2)}, u32[]{:S(2)}) collective-permute-start(bf16[4,768,128]{2,1,0:T(8,128)(2,1)S(1)} %all-to-all-done.1.refs_8_.refs_0_), channel_id=1, source_target_pairs={{0,12},{1,19},{2,14},{3,17},{4,0},{5,23},{6,2},{7,21},{8,4},{9,27}... | collective-permute-start | bytes 2359304 | tf_op jit(solution)/shard_map/ppermute | solution.py:338
  57.5 0.1 stack.67.dest_ref
  57.6 3.5 %shard_map.112.refs_4_ = bf16[512,8192]{1,0:T(8,128)(2,1)S(1)} custom-call(bf16[64,8192]{1,0:T(8,128)(2,1)} %get-tuple-element.14.refs_0_, bf16[64,8192]{1,0:T(8,128)(2,1)} %get-tuple-element.15.refs_1_, bf16[64,8192]{1,0:T(8,128)(2,1)} %get-tuple-element.16.refs_2_, bf16[64,8192]{1,0:T(8,128)(2,1)} %copy-done, bf16[64,8192]{1,0:T(8,128)(2,1)} %copy-done.1, ...), custom_call_target="tpu_custom_call" | custom-call | bytes 16777216 | tf_op jit(solution)/shard_map/pallas_call | solution.py:183
  61.1 0.0 copy-start.2
  61.1 0.0 collective-permute-done.3.refs_1_
  61.1 7.8 %collective-permute-done.4.refs_2_ = bf16[4,768,128]{2,1,0:T(8,128)(2,1)S(1)} collective-permute-done((bf16[4,768,128]{2,1,0:T(8,128)(2,1)S(1)}, bf16[4,768,128]{2,1,0:T(8,128)(2,1)S(1)}, u32[]{:S(2)}, u32[]{:S(2)}) %collective-permute-start.4) | collective-permute-done | bytes 786464 | tf_op jit(solution)/shard_map/ppermute | solution.py:338
  68.9 0.1 collective-permute-done.5.refs_3_
  69.0 3.7 %shard_map.113 = (f32[16,3,4,128]{3,2,1,0:T(4,128)S(1)}, f32[128,128]{1,0:T(8,128)S(1)}) custom-call(s32[16]{0:T(128)S(1)} %stack.67.dest_ref, bf16[4,768,128]{2,1,0:T(8,128)(2,1)S(1)} %all-to-all-done.1.refs_8_.refs_0_, bf16[4,768,128]{2,1,0:T(8,128)(2,1)S(1)} %collective-permute-done.3.refs_1_, bf16[4,768,128]{2,1,0:T(8,128)(2,1)S(1)} %collective-permute-done.4.refs_2_, ...), custom_call_target="tpu_custom_call" | custom-call | flops 2147483648 | bytes 12582912 | tf_op jit(solution)/shard_map/pallas_call | solution.py:151
  72.8 11.2 %all_to_all.25 = f32[16,3,4,128]{3,2,1,0:T(4,128)S(1)} all-to-all(f32[16,3,4,128]{3,2,1,0:T(4,128)S(1)} %get-tuple-element.21), channel_id=1, replica_groups={{0,2,4,6,8,10,12,14,16,18,20,22,24,26,28,30},{1,3,5,7,9,11,13,15,17,19,..., dimensions={0} | all-to-all | bytes 196608 | tf_op jit(solution)/shard_map/all_to_all | solution.py:62
  84.0 15.1 %all_to_all.26 = f32[16,3,4,128]{3,2,1,0:T(4,128)S(1)} all-to-all(f32[16,3,4,128]{3,2,1,0:T(4,128)S(1)} %broadcast_in_dim.4), channel_id=1, replica_groups={{256,288,320,352,384,416,448,480,0,32,64,96,128,160,192,224},{257,289,3..., dimensions={0} | all-to-all | bytes 196608 | tf_op jit(solution)/shard_map/all_to_all | solution.py:62
  99.2 0.7 broadcast_in_dim.5
  99.9 12.3 %all-to-all-start.4 = ((f32[32,3,4,128]{3,2,1,0:T(4,128)}), f32[32,3,4,128]{3,2,1,0:T(4,128)S(1)}, u32[]{:S(2)}, u32[]{:S(2)}) async-start(f32[32,3,4,128]{3,2,1,0:T(4,128)} %broadcast_in_dim.5), calls=%async_computation.4 | async-start | bytes 393216 | tf_op jit(solution)/shard_map/all_to_all | solution.py:62
  112.2 0.0 copy-done.2
  112.2 0.1 reshape.12
  112.3 0.1 pad.4
  112.4 1.9 %all-gather = f32[256,128]{1,0:T(8,128)S(1)} all-gather(f32[128,128]{1,0:T(8,128)S(1)} %get-tuple-element.22), channel_id=2, replica_groups={{0,1},{2,3},{4,5},{6,7},{8,9},{10,11},{12,13},{14,15},{16,17},{18,19},{..., dimensions={0}, use_global_device_ids=true | all-gather | bytes 196608 | tf_op jit(solution)/shard_map/all_gather | solution.py:350
  114.3 1.6 %all-to-all-done.4 = f32[32,3,4,128]{3,2,1,0:T(4,128)S(1)} async-done(((f32[32,3,4,128]{3,2,1,0:T(4,128)}), f32[32,3,4,128]{3,2,1,0:T(4,128)S(1)}, u32[]{:S(2)}, u32[]{:S(2)}) %all-to-all-start.4) | async-done | bytes 196640 | tf_op jit(solution)/shard_map/all_to_all | solution.py:62
  115.9 1.6 %shard_map.114 = f32[3,8,4096]{2,1,0:T(8,128)} custom-call(f32[16,2,3,4,128]{4,3,2,1,0:T(4,128)S(1)} %bitcast.21, f32[2,128,128]{2,1,0:T(8,128)S(1)} %bitcast.22, s32[1,256]{1,0:T(1,128)S(1)} %bitcast.23), custom_call_target="tpu_custom_call" | custom-call | flops 150994944 | bytes 2097152 | tf_op jit(solution)/shard_map/pallas_call | solution.py:307
  (3 shorter events, 0.1 us)
Async XLA Ops:
  1.5 30.9 %all-to-all-start = ((bf16[32,24,128]{2,1,0:T(8,128)(2,1)}), bf16[32,24,128]{2,1,0:T(8,128)(2,1)S(1)}, u32[]{:S(2)}, u32[]{:S(2)}) async-start(bf16[32,24,128]{2,1,0:T(8,128)(2,1)} %shard_map.109), calls=%async_computation | async-start | bytes 393216 | tf_op jit(solution)/shard_map/all_to_all | solution.py:62
  25.8 11.8 %collective-permute-start = (bf16[64,8192]{1,0:T(8,128)(2,1)}, bf16[64,8192]{1,0:T(8,128)(2,1)S(1)}, u32[]{:S(2)}, u32[]{:S(2)}) collective-permute-start(bf16[64,8192]{1,0:T(8,128)(2,1)} %get-tuple-element.14.refs_0_), channel_id=1, source_target_pairs={{0,1},{1,0},{2,3},{3,2},{4,5},{5,4},{6,7},{7,6},{8,9},{9,8},{10,11... | collective-permute-start | bytes 3145736 | tf_op jit(solution)/shard_map/ppermute | solution.py:335
  28.1 9.5 %collective-permute-start.1 = (bf16[64,8192]{1,0:T(8,128)(2,1)}, bf16[64,8192]{1,0:T(8,128)(2,1)S(1)}, u32[]{:S(2)}, u32[]{:S(2)}) collective-permute-start(bf16[64,8192]{1,0:T(8,128)(2,1)} %get-tuple-element.15.refs_1_), channel_id=1, source_target_pairs={{0,1},{1,0},{2,3},{3,2},{4,5},{5,4},{6,7},{7,6},{8,9},{9,8},{10,11... | collective-permute-start | bytes 3145736 | tf_op jit(solution)/shard_map/ppermute | solution.py:335
  30.1 7.5 %collective-permute-start.2 = (bf16[64,8192]{1,0:T(8,128)(2,1)}, bf16[64,8192]{1,0:T(8,128)(2,1)}, u32[]{:S(2)}, u32[]{:S(2)}) collective-permute-start(bf16[64,8192]{1,0:T(8,128)(2,1)} %get-tuple-element.16.refs_2_), channel_id=1, source_target_pairs={{0,1},{1,0},{2,3},{3,2},{4,5},{5,4},{6,7},{7,6},{8,9},{9,8},{10,11... | collective-permute-start | bytes 3145736 | tf_op jit(solution)/shard_map/ppermute | solution.py:335
  33.4 12.5 %all-to-all-start.1 = ((bf16[4,768,128]{2,1,0:T(8,128)(2,1)}), bf16[4,768,128]{2,1,0:T(8,128)(2,1)S(1)}, u32[]{:S(2)}, u32[]{:S(2)}) async-start(bf16[4,768,128]{2,1,0:T(8,128)(2,1)} %shard_map.110), calls=%async_computation.1 | async-start | bytes 1572864 | tf_op jit(solution)/shard_map/all_to_all | solution.py:62
  37.6 1.0 copy-start
  37.6 8.3 %copy-start.1 = (bf16[64,8192]{1,0:T(8,128)(2,1)}, bf16[64,8192]{1,0:T(8,128)(2,1)S(1)}, u32[]{:S(2)}) copy-start(bf16[64,8192]{1,0:T(8,128)(2,1)S(1)} %collective-permute-done.1.refs_4_) | copy-start | bytes 3145732
  46.0 15.1 %collective-permute-start.3 = (bf16[4,768,128]{2,1,0:T(8,128)(2,1)S(1)}, bf16[4,768,128]{2,1,0:T(8,128)(2,1)S(1)}, u32[]{:S(2)}, u32[]{:S(2)}) collective-permute-start(bf16[4,768,128]{2,1,0:T(8,128)(2,1)S(1)} %all-to-all-done.1.refs_8_.refs_0_), channel_id=1, source_target_pairs={{0,8},{1,3},{2,10},{3,1},{4,12},{5,7},{6,14},{7,5},{8,0},{9,11},{1... | collective-permute-start | bytes 2359304 | tf_op jit(solution)/shard_map/ppermute | solution.py:338
  50.6 18.3 %collective-permute-start.4 = (bf16[4,768,128]{2,1,0:T(8,128)(2,1)S(1)}, bf16[4,768,128]{2,1,0:T(8,128)(2,1)S(1)}, u32[]{:S(2)}, u32[]{:S(2)}) collective-permute-start(bf16[4,768,128]{2,1,0:T(8,128)(2,1)S(1)} %all-to-all-done.1.refs_8_.refs_0_), channel_id=1, source_target_pairs={{0,4},{1,17},{2,6},{3,19},{4,8},{5,21},{6,10},{7,23},{8,12},{9,25}... | collective-permute-start | bytes 2359304 | tf_op jit(solution)/shard_map/ppermute | solution.py:338
  52.8 16.2 %collective-permute-start.5 = (bf16[4,768,128]{2,1,0:T(8,128)(2,1)S(1)}, bf16[4,768,128]{2,1,0:T(8,128)(2,1)S(1)}, u32[]{:S(2)}, u32[]{:S(2)}) collective-permute-start(bf16[4,768,128]{2,1,0:T(8,128)(2,1)S(1)} %all-to-all-done.1.refs_8_.refs_0_), channel_id=1, source_target_pairs={{0,12},{1,19},{2,14},{3,17},{4,0},{5,23},{6,2},{7,21},{8,4},{9,27}... | collective-permute-start | bytes 2359304 | tf_op jit(solution)/shard_map/ppermute | solution.py:338
  61.1 51.1 %copy-start.2 = (s32[192]{0:T(256)S(1)}, s32[192]{0:T(256)}, u32[]{:S(2)}) copy-start(s32[192]{0:T(256)} %param.21) | copy-start | bytes 2308
  99.9 16.0 %all-to-all-start.4 = ((f32[32,3,4,128]{3,2,1,0:T(4,128)}), f32[32,3,4,128]{3,2,1,0:T(4,128)S(1)}, u32[]{:S(2)}, u32[]{:S(2)}) async-start(f32[32,3,4,128]{3,2,1,0:T(4,128)} %broadcast_in_dim.5), calls=%async_computation.4 | async-start | bytes 393216 | tf_op jit(solution)/shard_map/all_to_all | solution.py:62

commit v6 on v5

--- a/solution.py
+++ b/solution.py
@@ -41,8 +41,8 @@
 Z_GROUPS = [[device(z, *s, c) for z in ORDER] for s in SITES for c in range(NC)]
 FIRST_GROUPS = x_groups(0) + y_groups(1)
 SECOND_GROUPS = y_groups(0) + x_groups(1)
-PLANE_GROUPS = [[device(z, *s, c) for s in SITES] for z in range(NZ) for c in range(NC)]
 LAST = [(xl, (y + NY // 2) % NY, 1 - xh) for xl, y, xh in SITES]
+PLANE_GROUPS = [[device(z, *s, c) for s in LAST] for z in range(NZ) for c in range(NC)]
 LAYER_GROUPS = [[device(z, *s, c) for s in LAST for c in range(NC)] for z in range(NZ)]
 PAIRS = [[2 * i, 2 * i + 1] for i in range(NZ * PLANE)]
 SWAP = [(i, i ^ 1) for i in range(NZ * PLANE * NC)]
@@ -271,7 +271,7 @@
         for c in range(NC):
             for r in range(3):
                 row = p * 12 + r * 4
-                s_ref[row : row + 4, c * 128 : c * 128 + 128] = f_ref[LAST.index(SITES[p]), c, r]
+                s_ref[row : row + 4, c * 128 : c * 128 + 128] = f_ref[p, c, r]
     known = jnp.concatenate([h_ref[0], h_ref[1]], axis=1)
     doc = lax.broadcasted_iota(jnp.int32, (DOCS, NC * 128), 0)
     inside = (ids_ref[...] == doc)[None]

time: 118 us -> 117 us (level)
  blocking collectives: 28.2 us -> 25.6 us
  starting transfers between devices: 54.4 us -> 55.9 us
    all_to_all x2, blocking collectives: 26.3 us -> 23.7 us  [exchange(): return lax.all_to_all(blocks, BOTH, 0, 0, axis_index_groups=groups)]
    all_to_all x3, starting transfers between devices: 36.7 us -> 38.2 us  [exchange(): return lax.all_to_all(blocks, BOTH, 0, 0, axis_index_groups=groups)]
where the time goes in v6:
time: 117 us; the launch traced here: 116 us
  starting transfers between devices  55.9 us (48%)
  blocking collectives  25.6 us (22%)
  waiting for transfers between devices  16.8 us (14%)
  Pallas kernels  15.4 us (13%)
  local copies, waits for them, and re-layouts  1.93 us (2%)
    all_to_all x3, starting transfers between devices, exchange(): return lax.all_to_all(blocks, BOTH, 0, 0, axis_index_groups=groups)  38.2 us
    all_to_all x2, blocking collectives, exchange(): return lax.all_to_all(blocks, BOTH, 0, 0, axis_index_groups=groups)  23.7 us
    ppermute x3, starting transfers between devices, local(): lax.ppermute(line, BOTH, ring(shift))  11.1 us
    all_to_all x3, waiting for transfers between devices, exchange(): return lax.all_to_all(blocks, BOTH, 0, 0, axis_index_groups=groups)  8.9 us
    ppermute x3, waiting for transfers between devices, local(): lax.ppermute(line, BOTH, ring(shift))  7.93 us
    ppermute x3, starting transfers between devices, local(): other = [lax.ppermute(part, BOTH, SWAP) for part in own]  6.58 us
    pallas_call x1, Pallas kernels, stack(): pl.pallas_call(stack_kernel, grid=(8192 // width,), in_specs=[weight] * 3...  4.19 us
    pallas_call x1, Pallas kernels, block(): pl.pallas_call(block_kernel, in_specs=[pl.BlockSpec(memory_space=pltpu.SM...  3.71 us
  transfers between devices with their start and end apart: 9, of which 4 were waited for; matrix products, arithmetic and copies ran while one was open for 0% of the time, Pallas kernels for 7%

profile of v6, /device:TPU:1, one launch (start us, length us, event | category | flops | bytes accessed | tf_op | source)
XLA Modules:
  0.0 116.4 jit_solution(13153643611515974648)
XLA Ops:
  0.0 1.5 %shard_map.109 = bf16[32,24,128]{2,1,0:T(8,128)(2,1)} custom-call(bf16[16,192]{1,0:T(8,128)(2,1)} %bitcast.24, bf16[16,192]{1,0:T(8,128)(2,1)} %bitcast.25), custom_call_target="tpu_custom_call" | custom-call | bytes 262144 | tf_op jit(solution)/shard_map/pallas_call | solution.py:262
  1.5 20.1 %all-to-all-start = ((bf16[32,24,128]{2,1,0:T(8,128)(2,1)}), bf16[32,24,128]{2,1,0:T(8,128)(2,1)S(1)}, u32[]{:S(2)}, u32[]{:S(2)}) async-start(bf16[32,24,128]{2,1,0:T(8,128)(2,1)} %shard_map.109), calls=%async_computation | async-start | bytes 393216 | tf_op jit(solution)/shard_map/all_to_all | solution.py:62
  21.6 4.2 %shard_map.111 = (bf16[64,8192]{1,0:T(8,128)(2,1)}, bf16[64,8192]{1,0:T(8,128)(2,1)}, bf16[64,8192]{1,0:T(8,128)(2,1)}) custom-call(bf16[56,8192]{1,0:T(8,128)(2,1)} %refs_0_.1, bf16[56,8192]{1,0:T(8,128)(2,1)} %refs_1_.1, bf16[56,8192]{1,0:T(8,128)(2,1)} %refs_2_.1, bf16[56,64]{1,0:T(8,128)(2,1)} %refs_3_.1, bf16[56,64]{1,0:T(8,128)(2,1)} %refs_4_.1, ...), custom_call_target="tpu_custom_call" | custom-call | bytes 6291456 | tf_op jit(solution)/shard_map/pallas_call | solution.py:211
  25.8 2.3 %collective-permute-start = (bf16[64,8192]{1,0:T(8,128)(2,1)}, bf16[64,8192]{1,0:T(8,128)(2,1)S(1)}, u32[]{:S(2)}, u32[]{:S(2)}) collective-permute-start(bf16[64,8192]{1,0:T(8,128)(2,1)} %get-tuple-element.14.refs_0_), channel_id=1, source_target_pairs={{0,1},{1,0},{2,3},{3,2},{4,5},{5,4},{6,7},{7,6},{8,9},{9,8},{10,11... | collective-permute-start | bytes 3145736 | tf_op jit(solution)/shard_map/ppermute | solution.py:335
  28.1 2.1 %collective-permute-start.1 = (bf16[64,8192]{1,0:T(8,128)(2,1)}, bf16[64,8192]{1,0:T(8,128)(2,1)S(1)}, u32[]{:S(2)}, u32[]{:S(2)}) collective-permute-start(bf16[64,8192]{1,0:T(8,128)(2,1)} %get-tuple-element.15.refs_1_), channel_id=1, source_target_pairs={{0,1},{1,0},{2,3},{3,2},{4,5},{5,4},{6,7},{7,6},{8,9},{9,8},{10,11... | collective-permute-start | bytes 3145736 | tf_op jit(solution)/shard_map/ppermute | solution.py:335
  30.1 2.3 %collective-permute-start.2 = (bf16[64,8192]{1,0:T(8,128)(2,1)}, bf16[64,8192]{1,0:T(8,128)(2,1)}, u32[]{:S(2)}, u32[]{:S(2)}) collective-permute-start(bf16[64,8192]{1,0:T(8,128)(2,1)} %get-tuple-element.16.refs_2_), channel_id=1, source_target_pairs={{0,1},{1,0},{2,3},{3,2},{4,5},{5,4},{6,7},{7,6},{8,9},{9,8},{10,11... | collective-permute-start | bytes 3145736 | tf_op jit(solution)/shard_map/ppermute | solution.py:335
  32.4 0.0 all-to-all-done.column_ref
  32.4 1.0 shard_map.110
  33.4 4.2 %all-to-all-start.1 = ((bf16[4,768,128]{2,1,0:T(8,128)(2,1)}), bf16[4,768,128]{2,1,0:T(8,128)(2,1)S(1)}, u32[]{:S(2)}, u32[]{:S(2)}) async-start(bf16[4,768,128]{2,1,0:T(8,128)(2,1)} %shard_map.110), calls=%async_computation.1 | async-start | bytes 1572864 | tf_op jit(solution)/shard_map/all_to_all | solution.py:62
  37.6 0.0 collective-permute-done.refs_3_
  37.6 0.0 copy-start
  37.6 0.0 collective-permute-done.1.refs_4_
  37.6 0.0 copy-start.1
  37.6 0.0 collective-permute-done.2.refs_5_
  37.7 0.9 copy-done
  38.6 7.4 %all-to-all-done.1.refs_8_.refs_0_ = bf16[4,768,128]{2,1,0:T(8,128)(2,1)S(1)} async-done(((bf16[4,768,128]{2,1,0:T(8,128)(2,1)}), bf16[4,768,128]{2,1,0:T(8,128)(2,1)S(1)}, u32[]{:S(2)}, u32[]{:S(2)}) %all-to-all-start.1) | async-done | bytes 786464 | tf_op jit(solution)/shard_map/all_to_all | solution.py:62
  46.0 0.0 copy-done.1
  46.0 4.6 %collective-permute-start.3 = (bf16[4,768,128]{2,1,0:T(8,128)(2,1)S(1)}, bf16[4,768,128]{2,1,0:T(8,128)(2,1)S(1)}, u32[]{:S(2)}, u32[]{:S(2)}) collective-permute-start(bf16[4,768,128]{2,1,0:T(8,128)(2,1)S(1)} %all-to-all-done.1.refs_8_.refs_0_), channel_id=1, source_target_pairs={{0,8},{1,3},{2,10},{3,1},{4,12},{5,7},{6,14},{7,5},{8,0},{9,11},{1... | collective-permute-start | bytes 2359304 | tf_op jit(solution)/shard_map/ppermute | solution.py:338
  50.6 2.2 %collective-permute-start.4 = (bf16[4,768,128]{2,1,0:T(8,128)(2,1)S(1)}, bf16[4,768,128]{2,1,0:T(8,128)(2,1)S(1)}, u32[]{:S(2)}, u32[]{:S(2)}) collective-permute-start(bf16[4,768,128]{2,1,0:T(8,128)(2,1)S(1)} %all-to-all-done.1.refs_8_.refs_0_), channel_id=1, source_target_pairs={{0,4},{1,17},{2,6},{3,19},{4,8},{5,21},{6,10},{7,23},{8,12},{9,25}... | collective-permute-start | bytes 2359304 | tf_op jit(solution)/shard_map/ppermute | solution.py:338
  52.8 4.3 %collective-permute-start.5 = (bf16[4,768,128]{2,1,0:T(8,128)(2,1)S(1)}, bf16[4,768,128]{2,1,0:T(8,128)(2,1)S(1)}, u32[]{:S(2)}, u32[]{:S(2)}) collective-permute-start(bf16[4,768,128]{2,1,0:T(8,128)(2,1)S(1)} %all-to-all-done.1.refs_8_.refs_0_), channel_id=1, source_target_pairs={{0,12},{1,19},{2,14},{3,17},{4,0},{5,23},{6,2},{7,21},{8,4},{9,27}... | collective-permute-start | bytes 2359304 | tf_op jit(solution)/shard_map/ppermute | solution.py:338
  57.5 0.1 stack.67.dest_ref
  57.6 3.5 %shard_map.112.refs_4_ = bf16[512,8192]{1,0:T(8,128)(2,1)S(1)} custom-call(bf16[64,8192]{1,0:T(8,128)(2,1)} %get-tuple-element.14.refs_0_, bf16[64,8192]{1,0:T(8,128)(2,1)} %get-tuple-element.15.refs_1_, bf16[64,8192]{1,0:T(8,128)(2,1)} %get-tuple-element.16.refs_2_, bf16[64,8192]{1,0:T(8,128)(2,1)} %copy-done, bf16[64,8192]{1,0:T(8,128)(2,1)} %copy-done.1, ...), custom_call_target="tpu_custom_call" | custom-call | bytes 16777216 | tf_op jit(solution)/shard_map/pallas_call | solution.py:183
  61.1 0.0 copy-start.2
  61.1 0.0 collective-permute-done.3.refs_1_
  61.1 7.8 %collective-permute-done.4.refs_2_ = bf16[4,768,128]{2,1,0:T(8,128)(2,1)S(1)} collective-permute-done((bf16[4,768,128]{2,1,0:T(8,128)(2,1)S(1)}, bf16[4,768,128]{2,1,0:T(8,128)(2,1)S(1)}, u32[]{:S(2)}, u32[]{:S(2)}) %collective-permute-start.4) | collective-permute-done | bytes 786464 | tf_op jit(solution)/shard_map/ppermute | solution.py:338
  68.9 0.1 collective-permute-done.5.refs_3_
  69.0 3.7 %shard_map.113 = (f32[16,3,4,128]{3,2,1,0:T(4,128)S(1)}, f32[128,128]{1,0:T(8,128)S(1)}) custom-call(s32[16]{0:T(128)S(1)} %stack.67.dest_ref, bf16[4,768,128]{2,1,0:T(8,128)(2,1)S(1)} %all-to-all-done.1.refs_8_.refs_0_, bf16[4,768,128]{2,1,0:T(8,128)(2,1)S(1)} %collective-permute-done.3.refs_1_, bf16[4,768,128]{2,1,0:T(8,128)(2,1)S(1)} %collective-permute-done.4.refs_2_, ...), custom_call_target="tpu_custom_call" | custom-call | flops 2147483648 | bytes 12582912 | tf_op jit(solution)/shard_map/pallas_call | solution.py:151
  72.8 8.6 %all_to_all.25 = f32[16,3,4,128]{3,2,1,0:T(4,128)S(1)} all-to-all(f32[16,3,4,128]{3,2,1,0:T(4,128)S(1)} %get-tuple-element.21), channel_id=1, replica_groups={{10,8,14,12,2,0,6,4,26,24,30,28,18,16,22,20},{11,9,15,13,3,1,7,5,27,25,..., dimensions={0} | all-to-all | bytes 196608 | tf_op jit(solution)/shard_map/all_to_all | solution.py:62
  81.4 15.1 %all_to_all.26 = f32[16,3,4,128]{3,2,1,0:T(4,128)S(1)} all-to-all(f32[16,3,4,128]{3,2,1,0:T(4,128)S(1)} %broadcast_in_dim.4), channel_id=1, replica_groups={{256,288,320,352,384,416,448,480,0,32,64,96,128,160,192,224},{257,289,3..., dimensions={0} | all-to-all | bytes 196608 | tf_op jit(solution)/shard_map/all_to_all | solution.py:62
  96.6 0.7 broadcast_in_dim.5
  97.3 13.9 %all-to-all-start.4 = ((f32[32,3,4,128]{3,2,1,0:T(4,128)}), f32[32,3,4,128]{3,2,1,0:T(4,128)S(1)}, u32[]{:S(2)}, u32[]{:S(2)}) async-start(f32[32,3,4,128]{3,2,1,0:T(4,128)} %broadcast_in_dim.5), calls=%async_computation.4 | async-start | bytes 393216 | tf_op jit(solution)/shard_map/all_to_all | solution.py:62
  111.2 0.0 copy-done.2
  111.2 0.1 reshape.12
  111.3 0.1 pad.4
  111.3 1.9 %all-gather = f32[256,128]{1,0:T(8,128)S(1)} all-gather(f32[128,128]{1,0:T(8,128)S(1)} %get-tuple-element.22), channel_id=2, replica_groups={{0,1},{2,3},{4,5},{6,7},{8,9},{10,11},{12,13},{14,15},{16,17},{18,19},{..., dimensions={0}, use_global_device_ids=true | all-gather | bytes 196608 | tf_op jit(solution)/shard_map/all_gather | solution.py:350
  113.2 1.5 %all-to-all-done.4 = f32[32,3,4,128]{3,2,1,0:T(4,128)S(1)} async-done(((f32[32,3,4,128]{3,2,1,0:T(4,128)}), f32[32,3,4,128]{3,2,1,0:T(4,128)S(1)}, u32[]{:S(2)}, u32[]{:S(2)}) %all-to-all-start.4) | async-done | bytes 196640 | tf_op jit(solution)/shard_map/all_to_all | solution.py:62
  114.8 1.6 %shard_map.114 = f32[3,8,4096]{2,1,0:T(8,128)} custom-call(f32[16,2,3,4,128]{4,3,2,1,0:T(4,128)S(1)} %bitcast.21, f32[2,128,128]{2,1,0:T(8,128)S(1)} %bitcast.22, s32[1,256]{1,0:T(1,128)S(1)} %bitcast.23), custom_call_target="tpu_custom_call" | custom-call | flops 150994944 | bytes 2097152 | tf_op jit(solution)/shard_map/pallas_call | solution.py:307
  (3 shorter events, 0.1 us)
Async XLA Ops:
  1.5 30.9 %all-to-all-start = ((bf16[32,24,128]{2,1,0:T(8,128)(2,1)}), bf16[32,24,128]{2,1,0:T(8,128)(2,1)S(1)}, u32[]{:S(2)}, u32[]{:S(2)}) async-start(bf16[32,24,128]{2,1,0:T(8,128)(2,1)} %shard_map.109), calls=%async_computation | async-start | bytes 393216 | tf_op jit(solution)/shard_map/all_to_all | solution.py:62
  25.8 11.8 %collective-permute-start = (bf16[64,8192]{1,0:T(8,128)(2,1)}, bf16[64,8192]{1,0:T(8,128)(2,1)S(1)}, u32[]{:S(2)}, u32[]{:S(2)}) collective-permute-start(bf16[64,8192]{1,0:T(8,128)(2,1)} %get-tuple-element.14.refs_0_), channel_id=1, source_target_pairs={{0,1},{1,0},{2,3},{3,2},{4,5},{5,4},{6,7},{7,6},{8,9},{9,8},{10,11... | collective-permute-start | bytes 3145736 | tf_op jit(solution)/shard_map/ppermute | solution.py:335
  28.1 9.5 %collective-permute-start.1 = (bf16[64,8192]{1,0:T(8,128)(2,1)}, bf16[64,8192]{1,0:T(8,128)(2,1)S(1)}, u32[]{:S(2)}, u32[]{:S(2)}) collective-permute-start(bf16[64,8192]{1,0:T(8,128)(2,1)} %get-tuple-element.15.refs_1_), channel_id=1, source_target_pairs={{0,1},{1,0},{2,3},{3,2},{4,5},{5,4},{6,7},{7,6},{8,9},{9,8},{10,11... | collective-permute-start | bytes 3145736 | tf_op jit(solution)/shard_map/ppermute | solution.py:335
  30.1 7.5 %collective-permute-start.2 = (bf16[64,8192]{1,0:T(8,128)(2,1)}, bf16[64,8192]{1,0:T(8,128)(2,1)}, u32[]{:S(2)}, u32[]{:S(2)}) collective-permute-start(bf16[64,8192]{1,0:T(8,128)(2,1)} %get-tuple-element.16.refs_2_), channel_id=1, source_target_pairs={{0,1},{1,0},{2,3},{3,2},{4,5},{5,4},{6,7},{7,6},{8,9},{9,8},{10,11... | collective-permute-start | bytes 3145736 | tf_op jit(solution)/shard_map/ppermute | solution.py:335
  33.4 12.5 %all-to-all-start.1 = ((bf16[4,768,128]{2,1,0:T(8,128)(2,1)}), bf16[4,768,128]{2,1,0:T(8,128)(2,1)S(1)}, u32[]{:S(2)}, u32[]{:S(2)}) async-start(bf16[4,768,128]{2,1,0:T(8,128)(2,1)} %shard_map.110), calls=%async_computation.1 | async-start | bytes 1572864 | tf_op jit(solution)/shard_map/all_to_all | solution.py:62
  37.6 1.0 copy-start
  37.6 8.3 %copy-start.1 = (bf16[64,8192]{1,0:T(8,128)(2,1)}, bf16[64,8192]{1,0:T(8,128)(2,1)S(1)}, u32[]{:S(2)}) copy-start(bf16[64,8192]{1,0:T(8,128)(2,1)S(1)} %collective-permute-done.1.refs_4_) | copy-start | bytes 3145732
  46.0 15.1 %collective-permute-start.3 = (bf16[4,768,128]{2,1,0:T(8,128)(2,1)S(1)}, bf16[4,768,128]{2,1,0:T(8,128)(2,1)S(1)}, u32[]{:S(2)}, u32[]{:S(2)}) collective-permute-start(bf16[4,768,128]{2,1,0:T(8,128)(2,1)S(1)} %all-to-all-done.1.refs_8_.refs_0_), channel_id=1, source_target_pairs={{0,8},{1,3},{2,10},{3,1},{4,12},{5,7},{6,14},{7,5},{8,0},{9,11},{1... | collective-permute-start | bytes 2359304 | tf_op jit(solution)/shard_map/ppermute | solution.py:338
  50.6 18.3 %collective-permute-start.4 = (bf16[4,768,128]{2,1,0:T(8,128)(2,1)S(1)}, bf16[4,768,128]{2,1,0:T(8,128)(2,1)S(1)}, u32[]{:S(2)}, u32[]{:S(2)}) collective-permute-start(bf16[4,768,128]{2,1,0:T(8,128)(2,1)S(1)} %all-to-all-done.1.refs_8_.refs_0_), channel_id=1, source_target_pairs={{0,4},{1,17},{2,6},{3,19},{4,8},{5,21},{6,10},{7,23},{8,12},{9,25}... | collective-permute-start | bytes 2359304 | tf_op jit(solution)/shard_map/ppermute | solution.py:338
  52.8 16.2 %collective-permute-start.5 = (bf16[4,768,128]{2,1,0:T(8,128)(2,1)S(1)}, bf16[4,768,128]{2,1,0:T(8,128)(2,1)S(1)}, u32[]{:S(2)}, u32[]{:S(2)}) collective-permute-start(bf16[4,768,128]{2,1,0:T(8,128)(2,1)S(1)} %all-to-all-done.1.refs_8_.refs_0_), channel_id=1, source_target_pairs={{0,12},{1,19},{2,14},{3,17},{4,0},{5,23},{6,2},{7,21},{8,4},{9,27}... | collective-permute-start | bytes 2359304 | tf_op jit(solution)/shard_map/ppermute | solution.py:338
  61.1 50.1 %copy-start.2 = (s32[192]{0:T(256)S(1)}, s32[192]{0:T(256)}, u32[]{:S(2)}) copy-start(s32[192]{0:T(256)} %param.21) | copy-start | bytes 2308
  97.3 17.5 %all-to-all-start.4 = ((f32[32,3,4,128]{3,2,1,0:T(4,128)}), f32[32,3,4,128]{3,2,1,0:T(4,128)S(1)}, u32[]{:S(2)}, u32[]{:S(2)}) async-start(f32[32,3,4,128]{3,2,1,0:T(4,128)} %broadcast_in_dim.5), calls=%async_computation.4 | async-start | bytes 393216 | tf_op jit(solution)/shard_map/all_to_all | solution.py:62
